TPU v7x, 32 devices: a whole 2x2x4 slice. The times are simulated.
32 devices in a mesh: batch: 8 (over z, y), head: 4 (over x, core).
Axes of the slice: x: 2, y: 2, z: 4, core: 2. Of those that a mesh axis runs over, the one named last changes fastest.
Arguments:
- frozen_input: bfloat16 [128, 128, 1024], P('batch', None, 'head'), may hold values from -6 to 6
- frozen_attend: bfloat16 [2, 3, 1024, 1024], P(None, None, None, 'head'), may hold values from -0.1875 to 0.1875
- frozen_output: bfloat16 [2, 1024, 1024], P(None, 'head'), may hold values from -0.75 to 0.75
- frozen_expand: bfloat16 [2, 1024, 4096], P(None, None, 'head'), may hold values from -0.1875 to 0.1875
- frozen_reduce: bfloat16 [2, 4096, 1024], P(None, 'head'), may hold values from -0.09375 to 0.09375
- frozen_gains: float32 [2, 2, 1024], replicated, may hold values from 0.5 to 1.5
- lengths: int32 [128, 7], P('batch'), may hold values from 20 to 128
- side_input: bfloat16 [128, 128, 128], P(('batch', 'head')), may hold values from -6 to 6
- cotangent: float32 [128, 128, 128], P(('batch', 'head')), may hold values from -12 to 12
- attend_master: float32 [1024, 128], P(('batch', 'head')), may hold values from -2 to 2
- attend_moment: float32 [1024, 128], P(('batch', 'head')), may hold values from -0.001953125 to 0.001953125
- attend_square: float32 [1024, 128], P(('batch', 'head')), may hold values from 3.8146972e-10 to 1.5258789e-09
- feed_master: float32 [512, 512], P(('batch', 'head')), may hold values from -0.5 to 0.5
- feed_moment: float32 [512, 512], P(('batch', 'head')), may hold values from -0.001953125 to 0.001953125
- feed_square: float32 [512, 512], P(('batch', 'head')), may hold values from 3.8146972e-10 to 1.5258789e-09
- down_master: float32 [2048, 128], P(('batch', 'head')), may hold values from -0.1875 to 0.1875
- down_moment: float32 [2048, 128], P(('batch', 'head')), may hold values from -0.001953125 to 0.001953125
- down_square: float32 [2048, 128], P(('batch', 'head')), may hold values from 3.8146972e-10 to 1.5258789e-09
- gains_master: float32 [6, 128], replicated, may hold values from 0.5 to 1.5
- gains_moment: float32 [6, 128], replicated, may hold values from -0.0078125 to 0.0078125
- gains_square: float32 [6, 128], replicated, may hold values from 1.5258789e-09 to 6.1035155e-09
Outputs:
- side_output: float32 [128, 128, 128], P(('batch', 'head'))
- input_grad: float32 [128, 128, 128], P(('batch', 'head'))
- grad_norm: float32 [], replicated
- attend_new: float32 [1024, 128], P(('batch', 'head'))
- attend_first: float32 [1024, 128], P(('batch', 'head'))
- attend_second: float32 [1024, 128], P(('batch', 'head'))
- attend_copy: bfloat16 [1024, 128], P(('batch', 'head'))
- feed_new: float32 [512, 512], P(('batch', 'head'))
- feed_first: float32 [512, 512], P(('batch', 'head'))
- feed_second: float32 [512, 512], P(('batch', 'head'))
- feed_copy: bfloat16 [512, 512], P(('batch', 'head'))
- down_new: float32 [2048, 128], P(('batch', 'head'))
- down_first: float32 [2048, 128], P(('batch', 'head'))
- down_second: float32 [2048, 128], P(('batch', 'head'))
- down_copy: bfloat16 [2048, 128], P(('batch', 'head'))
- gains_new: float32 [6, 128], replicated
- gains_first: float32 [6, 128], replicated
- gains_second: float32 [6, 128], replicated
All inputs are finite; a program needn't handle non-finite values.
Results may differ from a plain program's by a relative error of at most 0.03.
Values may be sent and summed in bfloat16 or wider, within the bound.
No kernel may reach another device: no remote copies, remote signals or barrier semaphores. Data moves between devices by JAX's collectives and lax.ppermute only.
A program may use at most 128 MiB of HBM per device.

v0:
```python
from functools import partial

import jax
import jax.numpy as jnp
from jax import lax
from jax.sharding import PartitionSpec as P

D = 1024
HEAD_DIM = 64
S = 128
SIDE_HD = 8
SF = 512
L = 2
ROW = 128
STEP = 10


NORM_EPS = 1e-06
THRESHOLD = 1.0
BETA_ONE = 0.9
BETA_TWO = 0.999
ADAM_EPS = 1e-08
RATE_MATRIX = 0.12
RATE_SMALL = 0.5
WEIGHT_DECAY = 0.01
MASKED = -1e30


def root_norm(values, gains):
    return values * lax.rsqrt(jnp.mean(values * values, axis=-1, keepdims=True) + NORM_EPS) * gains


def norm_scale(values):
    return lax.rsqrt(jnp.mean(values * values, axis=-1, keepdims=True) + NORM_EPS)


def norm_back(values, scale, gains, grad_normed):
    weighted = grad_normed * gains
    grad_values = scale * weighted - values * scale**3 * jnp.mean(
        weighted * values, axis=-1, keepdims=True
    )
    grad_gains = jnp.sum(grad_normed * values * scale, axis=(0, 1))
    return (grad_values, grad_gains)


def segments(lengths):
    sent_ends = jnp.cumsum(lengths, axis=-1)
    kept_flag = sent_ends <= ROW
    places = jnp.arange(ROW, dtype=jnp.int32)
    labels = jnp.sum(
        (kept_flag[:, None, :] & (sent_ends[:, None, :] <= places[None, :, None])).astype(
            jnp.int32
        ),
        axis=-1,
    )
    filled = jnp.sum(jnp.where(kept_flag, lengths, 0), axis=-1)
    real_tok = (places[None, :] < filled[:, None]).astype(jnp.float32)
    return (labels[:, :, None] == labels[:, None, :], real_tok)


def backbone_attention(normed, w_attend, same_seg):
    col_count = w_attend.shape[2]
    projected = jnp.einsum(
        "rtd,jdc->jrtc", normed, w_attend, preferred_element_type=jnp.float32
    ).astype(jnp.bfloat16)
    head_shape = normed.shape[:2] + (col_count // HEAD_DIM, HEAD_DIM)
    queries = projected[0].reshape(head_shape)
    key_rows = projected[1].reshape(head_shape)
    value_rows = projected[2].reshape(head_shape)
    scores = jnp.einsum(
        "rqhc,rkhc->rhqk", queries, key_rows, preferred_element_type=jnp.float32
    ) * HEAD_DIM ** (-0.5)
    scores = jnp.where(same_seg[:, None], scores, MASKED)
    shares = jax.nn.softmax(scores, axis=-1).astype(jnp.bfloat16)
    context = jnp.einsum("rhqk,rkhc->rqhc", shares, value_rows, preferred_element_type=jnp.float32)
    return context.astype(jnp.bfloat16).reshape(normed.shape[:2] + (col_count,))


def attend_part(normed, w_attend, w_output, same_seg):
    context = backbone_attention(normed, w_attend, same_seg)
    return jnp.einsum("rtc,cd->rtd", context, w_output, preferred_element_type=jnp.float32)


def feed_part(normed, w_expand, w_reduce):
    inner = jax.nn.gelu(
        jnp.einsum("rtd,df->rtf", normed, w_expand, preferred_element_type=jnp.float32)
    ).astype(jnp.bfloat16)
    return jnp.einsum("rtf,fd->rtd", inner, w_reduce, preferred_element_type=jnp.float32)


def head_sublayer(hidden, gains, work):
    whole = lax.all_gather(hidden, "head", axis=2, tiled=True)
    normed = root_norm(whole.astype(jnp.float32), gains).astype(jnp.bfloat16)
    summed = lax.psum_scatter(
        work(normed).astype(jnp.bfloat16), "head", scatter_dimension=2, tiled=True
    ).astype(jnp.float32)
    return (hidden.astype(jnp.float32) + summed).astype(jnp.bfloat16)


def side_forward(tapped, side_state, mats, feeds, smalls, same_seg):
    head_shape = side_state.shape[:2] + (S // SIDE_HD, SIDE_HD)
    gating = jax.nn.sigmoid(smalls[2])
    mixed = gating * tapped + (1.0 - gating) * side_state
    first_scale = norm_scale(mixed)
    normed = (mixed * first_scale * smalls[0]).astype(jnp.bfloat16)
    projected = jnp.einsum(
        "rts,jsc->jrtc", normed, mats[:3], preferred_element_type=jnp.float32
    ).astype(jnp.bfloat16)
    queries = projected[0].reshape(head_shape)
    key_rows = projected[1].reshape(head_shape)
    value_rows = projected[2].reshape(head_shape)
    scores = jnp.einsum(
        "rqhc,rkhc->rhqk", queries, key_rows, preferred_element_type=jnp.float32
    ) * SIDE_HD ** (-0.5)
    scores = jnp.where(same_seg[:, None], scores, MASKED)
    highest = jnp.max(scores, axis=-1, keepdims=True)
    total_log = highest + jnp.log(jnp.sum(jnp.exp(scores - highest), axis=-1, keepdims=True))
    shares = jnp.exp(scores - total_log).astype(jnp.bfloat16)
    context = (
        jnp.einsum("rhqk,rkhc->rqhc", shares, value_rows, preferred_element_type=jnp.float32)
        .astype(jnp.bfloat16)
        .reshape(side_state.shape)
    )
    middle = mixed + jnp.einsum("rtc,cs->rts", context, mats[3], preferred_element_type=jnp.float32)
    second_scale = norm_scale(middle)
    normed_two = (middle * second_scale * smalls[1]).astype(jnp.bfloat16)
    inner = jnp.einsum("rts,sf->rtf", normed_two, feeds[0], preferred_element_type=jnp.float32)
    active = jax.nn.gelu(inner).astype(jnp.bfloat16)
    result = middle + jnp.einsum(
        "rtf,sf->rts", active, feeds[1], preferred_element_type=jnp.float32
    )
    kept_all = (
        tapped,
        side_state,
        mixed,
        first_scale,
        normed,
        queries,
        key_rows,
        value_rows,
        total_log,
        context,
        middle,
        second_scale,
        normed_two,
        inner,
        active,
    )
    return (result, kept_all)


def side_backward(kept_all, grad_out, mats, feeds, smalls, same_seg):
    (
        tapped,
        side_state,
        mixed,
        first_scale,
        normed,
        queries,
        key_rows,
        value_rows,
        total_log,
        context,
        middle,
        second_scale,
        normed_two,
        inner,
        active,
    ) = kept_all
    head_shape = queries.shape
    grad_outer = grad_out.astype(jnp.bfloat16)
    grad_feed_out = jnp.einsum(
        "rts,rtf->sf", grad_outer, active, preferred_element_type=jnp.float32
    )
    grad_active = jnp.einsum(
        "rts,sf->rtf", grad_outer, feeds[1], preferred_element_type=jnp.float32
    )
    unused_value, gelu_back = jax.vjp(jax.nn.gelu, inner)
    grad_inner = gelu_back(grad_active)[0].astype(jnp.bfloat16)
    grad_feed_in = jnp.einsum(
        "rts,rtf->sf", normed_two, grad_inner, preferred_element_type=jnp.float32
    )
    grad_normed_two = jnp.einsum(
        "rtf,sf->rts", grad_inner, feeds[0], preferred_element_type=jnp.float32
    )
    grad_middle, grad_gain_two = norm_back(middle, second_scale, smalls[1], grad_normed_two)
    grad_middle = grad_middle + grad_out
    grad_branch = grad_middle.astype(jnp.bfloat16)
    grad_mat_out = jnp.einsum(
        "rtc,rts->cs", context, grad_branch, preferred_element_type=jnp.float32
    )
    grad_context = (
        jnp.einsum("rts,cs->rtc", grad_branch, mats[3], preferred_element_type=jnp.float32)
        .astype(jnp.bfloat16)
        .reshape(head_shape)
    )
    scores = jnp.einsum(
        "rqhc,rkhc->rhqk", queries, key_rows, preferred_element_type=jnp.float32
    ) * SIDE_HD ** (-0.5)
    scores = jnp.where(same_seg[:, None], scores, MASKED)
    shares = jnp.exp(scores - total_log)
    grad_shares = jnp.einsum(
        "rqhc,rkhc->rhqk", grad_context, value_rows, preferred_element_type=jnp.float32
    )
    grad_values = jnp.einsum(
        "rhqk,rqhc->rkhc",
        shares.astype(jnp.bfloat16),
        grad_context,
        preferred_element_type=jnp.float32,
    ).astype(jnp.bfloat16)
    grad_scores = (
        shares * (grad_shares - jnp.sum(shares * grad_shares, axis=-1, keepdims=True))
    ).astype(jnp.bfloat16)
    grad_queries = (
        jnp.einsum("rhqk,rkhc->rqhc", grad_scores, key_rows, preferred_element_type=jnp.float32)
        * SIDE_HD ** (-0.5)
    ).astype(jnp.bfloat16)
    grad_keys = (
        jnp.einsum("rhqk,rqhc->rkhc", grad_scores, queries, preferred_element_type=jnp.float32)
        * SIDE_HD ** (-0.5)
    ).astype(jnp.bfloat16)
    grad_proj = jnp.stack([grad_queries, grad_keys, grad_values]).reshape((3,) + mixed.shape)
    grad_mats_in = jnp.einsum(
        "rts,jrtc->jsc", normed, grad_proj, preferred_element_type=jnp.float32
    )
    grad_normed = jnp.einsum(
        "jrtc,jsc->rts", grad_proj, mats[:3], preferred_element_type=jnp.float32
    )
    grad_mixed, grad_gain_one = norm_back(mixed, first_scale, smalls[0], grad_normed)
    grad_mixed = grad_mixed + grad_middle
    gating = jax.nn.sigmoid(smalls[2])
    grad_tap = (gating * grad_mixed).astype(jnp.bfloat16)
    grad_state = (1.0 - gating) * grad_mixed
    grad_gate = jnp.sum(grad_mixed * (tapped - side_state), axis=(0, 1)) * gating * (1.0 - gating)
    grad_mats = jnp.concatenate([grad_mats_in, grad_mat_out[None]], axis=0)
    grad_feeds = jnp.stack([grad_feed_in, grad_feed_out])
    grad_smalls = jnp.stack([grad_gain_one, grad_gain_two, grad_gate])
    return (grad_state, grad_tap, grad_mats, grad_feeds, grad_smalls)


def adamw(master, moment, square, grad_now, clip, rate, decay):
    grad_now = grad_now * clip
    moment = BETA_ONE * moment + (1.0 - BETA_ONE) * grad_now
    square = BETA_TWO * square + (1.0 - BETA_TWO) * grad_now * grad_now
    first_hat = moment / (1.0 - BETA_ONE**STEP)
    second_hat = square / (1.0 - BETA_TWO**STEP)
    master = master - rate * (first_hat / (jnp.sqrt(second_hat) + ADAM_EPS) + decay * master)
    return (master, moment, square)


def shards(
    frozen_input,
    frozen_attend,
    frozen_output,
    frozen_expand,
    frozen_reduce,
    frozen_gains,
    lengths,
    side_input,
    cotangent,
    attend_master,
    attend_moment,
    attend_square,
    feed_master,
    feed_moment,
    feed_square,
    down_master,
    down_moment,
    down_square,
    gains_master,
    gains_moment,
    gains_square,
):
    head_count = lax.axis_size("head")
    head_place = lax.axis_index("head")
    own_rows = lengths.shape[0] // head_count
    own_lengths = lax.dynamic_slice_in_dim(lengths, head_place * own_rows, own_rows, 0)
    same_seg, real_tok = segments(own_lengths)
    attend_full, feed_full, down_full = (
        lax.all_gather(attend_master.astype(jnp.bfloat16), ("batch", "head"), axis=0, tiled=True),
        lax.all_gather(feed_master.astype(jnp.bfloat16), ("batch", "head"), axis=0, tiled=True),
        lax.all_gather(down_master.astype(jnp.bfloat16), ("batch", "head"), axis=0, tiled=True),
    )
    mats_all = attend_full.reshape(L, 4, S, S)
    feeds_all = feed_full.reshape(L, 2, S, SF)
    downs = down_full.reshape(L, D, S)
    smalls_all = gains_master.reshape(L, 3, S)
    tapped_rows = []
    same_all, unused_real = segments(lengths)
    hidden = frozen_input
    for layer_at in range(L):
        hidden = head_sublayer(
            hidden,
            frozen_gains[layer_at, 0],
            partial(
                attend_part,
                w_attend=frozen_attend[layer_at],
                w_output=frozen_output[layer_at],
                same_seg=same_all,
            ),
        )
        hidden = head_sublayer(
            hidden,
            frozen_gains[layer_at, 1],
            partial(feed_part, w_expand=frozen_expand[layer_at], w_reduce=frozen_reduce[layer_at]),
        )
        tapped_rows.append(lax.all_to_all(hidden, "head", split_axis=0, concat_axis=2, tiled=True))
    side_state = side_input.astype(jnp.float32)
    kept_layers = []
    for layer_at in range(L):
        tapped = jnp.einsum(
            "rtd,ds->rts",
            tapped_rows[layer_at],
            downs[layer_at],
            preferred_element_type=jnp.float32,
        )
        side_state, kept_all = side_forward(
            tapped,
            side_state,
            mats_all[layer_at],
            feeds_all[layer_at],
            smalls_all[layer_at],
            same_seg,
        )
        kept_layers.append(kept_all)
    grad_now = cotangent * real_tok[:, :, None]
    mats_list, feeds_list, downs_list, smalls_list = ([], [], [], [])
    for layer_at in reversed(range(L)):
        grad_now, grad_tap, grad_mats, grad_feeds, grad_smalls = side_backward(
            kept_layers[layer_at],
            grad_now,
            mats_all[layer_at],
            feeds_all[layer_at],
            smalls_all[layer_at],
            same_seg,
        )
        downs_list.append(
            jnp.einsum(
                "rtd,rts->ds", tapped_rows[layer_at], grad_tap, preferred_element_type=jnp.float32
            )
        )
        mats_list.append(grad_mats)
        feeds_list.append(grad_feeds)
        smalls_list.append(grad_smalls)
    grad_attend = jnp.stack(mats_list[::-1]).reshape(L * 4 * S, S)
    grad_feed = jnp.stack(feeds_list[::-1]).reshape(L * 2 * S, SF)
    grad_down = jnp.stack(downs_list[::-1]).reshape(L * D, S)
    grad_gains = jnp.stack(smalls_list[::-1]).reshape(L * 3, S)
    grad_attend, grad_feed, grad_down, grad_gains = lax.psum(
        (grad_attend, grad_feed, grad_down, grad_gains), ("batch", "head")
    )
    squares = (
        jnp.sum(grad_attend * grad_attend)
        + jnp.sum(grad_feed * grad_feed)
        + jnp.sum(grad_down * grad_down)
        + jnp.sum(grad_gains * grad_gains)
    )
    member = lax.axis_index(("batch", "head"))
    portions = [
        lax.dynamic_slice_in_dim(summed, member * owned.shape[0], owned.shape[0], 0)
        for summed, owned in (
            (grad_attend, attend_master),
            (grad_feed, feed_master),
            (grad_down, down_master),
        )
    ]
    grad_norm = jnp.sqrt(squares)
    clip = jnp.minimum(1.0, THRESHOLD / grad_norm)
    attend_new, attend_first, attend_second = adamw(
        attend_master, attend_moment, attend_square, portions[0], clip, RATE_MATRIX, WEIGHT_DECAY
    )
    feed_new, feed_first, feed_second = adamw(
        feed_master, feed_moment, feed_square, portions[1], clip, RATE_MATRIX, WEIGHT_DECAY
    )
    down_new, down_first, down_second = adamw(
        down_master, down_moment, down_square, portions[2], clip, RATE_MATRIX, WEIGHT_DECAY
    )
    gains_new, gains_first, gains_second = adamw(
        gains_master, gains_moment, gains_square, grad_gains, clip, RATE_SMALL, 0.0
    )
    return (
        side_state,
        grad_now,
        grad_norm,
        attend_new,
        attend_first,
        attend_second,
        attend_new.astype(jnp.bfloat16),
        feed_new,
        feed_first,
        feed_second,
        feed_new.astype(jnp.bfloat16),
        down_new,
        down_first,
        down_second,
        down_new.astype(jnp.bfloat16),
        gains_new,
        gains_first,
        gains_second,
    )


def solution(mesh):
    return jax.shard_map(
        shards,
        mesh=mesh,
        in_specs=(
            P("batch", None, "head"),
            P(None, None, None, "head"),
            P(None, "head", None),
            P(None, None, "head"),
            P(None, "head", None),
            P(),
            P("batch", None),
            P(("batch", "head"), None, None),
            P(("batch", "head"), None, None),
            P(("batch", "head"), None),
            P(("batch", "head"), None),
            P(("batch", "head"), None),
            P(("batch", "head"), None),
            P(("batch", "head"), None),
            P(("batch", "head"), None),
            P(("batch", "head"), None),
            P(("batch", "head"), None),
            P(("batch", "head"), None),
            P(),
            P(),
            P(),
        ),
        out_specs=(
            P(("batch", "head"), None, None),
            P(("batch", "head"), None, None),
            P(),
            P(("batch", "head"), None),
            P(("batch", "head"), None),
            P(("batch", "head"), None),
            P(("batch", "head"), None),
            P(("batch", "head"), None),
            P(("batch", "head"), None),
            P(("batch", "head"), None),
            P(("batch", "head"), None),
            P(("batch", "head"), None),
            P(("batch", "head"), None),
            P(("batch", "head"), None),
            P(("batch", "head"), None),
            P(),
            P(),
            P(),
        ),
        check_vma=False,
    )
```

profile of v0, /device:TPU:0, one launch (start us, length us, event | category | flops | bytes accessed | tf_op | source)
XLA Modules:
  0.0 752.1 jit_solution(750991506079300261)
XLA Ops:
  9.9 37.4 %all-gather.5.cloned.1.call-done = bf16[16,128,1024]{2,1,0:T(8,128)(2,1)} async-done(((bf16[16,128,256]{2,1,0:T(8,128)(2,1)}), bf16[16,128,1024]{2,1,0:T(8,128)(2,1)}) %all-gather.5.cloned.1.call-update) | async-done | bytes 4194320 | tf_op jit(solution)/shard_map/all_gather | solution.py:92
  47.3 3.2 fusion.2
  50.8 5.1 convert_bitcast_fusion.1
  59.4 4.8 fusion.226
  64.2 3.0 fusion.113
  67.2 3.2 convolution_convert_fusion.1
  70.5 44.6 %reduce-scatter.5.cloned.1.call-done = bf16[16,128,256]{2,1,0:T(8,128)(2,1)} async-done(((bf16[16,128,1024]{2,1,0:T(8,128)(2,1)}), bf16[16,128,256]{2,1,0:T(8,128)(2,1)}) %reduce-scatter.5.cloned.1.call-update) | async-done | bytes 1048592 | tf_op jit(solution)/shard_map/reduce_scatter | solution.py:94
  115.2 2.6 add_convert_fusion.3
  118.3 34.7 %all-gather.7.cloned.1.call-done = bf16[16,128,1024]{2,1,0:T(8,128)(2,1)} async-done(((bf16[16,128,256]{2,1,0:T(8,128)(2,1)}), bf16[16,128,1024]{2,1,0:T(8,128)(2,1)}) %all-gather.7.cloned.1.call-update) | async-done | bytes 4194320 | tf_op jit(solution)/shard_map/all_gather | solution.py:92
  153.0 3.1 fusion.5
  156.1 13.5 %fusion.64 = bf16[16,128,1024]{2,1,0:T(8,128)(2,1)} fusion(bf16[2,1024,1024]{2,1,0:T(8,128)(2,1)} %param.25, bf16[16,128,1024]{2,1,0:T(8,128)(2,1)} %all-gather.7.cloned.1.call-done, f32[1024]{0:T(1024)S(1)} %bitcast.371, f32[16,128]{1,0:T(8,128)S(1)} %add_rsqrt_fusion.2, bf16[2,1024,1024]{2,1,0:T(8,128)(2,1)} %param.24), kind=kOutput, calls=%fused_computation.86 | convolution fusion | flops 8619294720 | bytes 12595200 | tf_op jit(solution)/shard_map/rtf,fd->rtd/dot_general | solution.py:88
  169.6 44.6 %reduce-scatter.7.cloned.1.call-done = bf16[16,128,256]{2,1,0:T(8,128)(2,1)} async-done(((bf16[16,128,1024]{2,1,0:T(8,128)(2,1)}), bf16[16,128,256]{2,1,0:T(8,128)(2,1)}) %reduce-scatter.7.cloned.1.call-update) | async-done | bytes 1048592 | tf_op jit(solution)/shard_map/reduce_scatter | solution.py:94
  214.2 2.6 add_convert_fusion.2
  216.9 35.1 %all-gather.9.cloned.1.call-done = bf16[16,128,1024]{2,1,0:T(8,128)(2,1)} async-done(((bf16[16,128,256]{2,1,0:T(8,128)(2,1)}), bf16[16,128,1024]{2,1,0:T(8,128)(2,1)}) %all-gather.9.cloned.1.call-update) | async-done | bytes 4194320 | tf_op jit(solution)/shard_map/all_gather | solution.py:92
  252.0 3.2 fusion.8
  255.5 5.1 convert_bitcast_fusion
  264.1 4.8 fusion.227
  269.0 3.0 fusion.112
  271.9 3.2 convolution_convert_fusion
  275.4 44.4 %reduce-scatter.9.cloned.1.call-done = bf16[16,128,256]{2,1,0:T(8,128)(2,1)} async-done(((bf16[16,128,1024]{2,1,0:T(8,128)(2,1)}), bf16[16,128,256]{2,1,0:T(8,128)(2,1)}) %reduce-scatter.9.cloned.1.call-update) | async-done | bytes 1048592 | tf_op jit(solution)/shard_map/reduce_scatter | solution.py:94
  319.8 2.8 add_convert_fusion.1
  322.8 35.1 %all-gather.11.cloned.1.call-done = bf16[16,128,1024]{2,1,0:T(8,128)(2,1)} async-done(((bf16[16,128,256]{2,1,0:T(8,128)(2,1)}), bf16[16,128,1024]{2,1,0:T(8,128)(2,1)}) %all-gather.11.cloned.1.call-update) | async-done | bytes 4194320 | tf_op jit(solution)/shard_map/all_gather | solution.py:92
  357.9 3.1 fusion.11
  361.0 13.5 %fusion.67 = bf16[16,128,1024]{2,1,0:T(8,128)(2,1)} fusion(bf16[2,1024,1024]{2,1,0:T(8,128)(2,1)} %param.25, bf16[16,128,1024]{2,1,0:T(8,128)(2,1)} %all-gather.11.cloned.1.call-done, f32[1024]{0:T(1024)S(1)} %bitcast.369, f32[16,128]{1,0:T(8,128)S(1)} %add_rsqrt_fusion, bf16[2,1024,1024]{2,1,0:T(8,128)(2,1)} %param.24), kind=kOutput, calls=%fused_computation.87 | convolution fusion | flops 8619294720 | bytes 12595200 | tf_op jit(solution)/shard_map/rtf,fd->rtd/dot_general | solution.py:88
  377.3 3.6 all-to-all-start.1
  380.9 48.3 %all_gather.26 = bf16[1024,128]{1,0:T(8,128)(2,1)S(1)} all-gather(bf16[32,128]{1,0:T(8,128)(2,1)S(1)} %convert_element_type.304), channel_id=1, replica_groups=mesh['batch'=8,'head'=4] {'batch','head'}, dimensions={0}, use_global_device_ids=true | all-gather | bytes 270336 | tf_op jit(solution)/shard_map/all_gather | solution.py:280
  429.9 40.7 %all_gather.27 = bf16[512,512]{1,0:T(8,128)(2,1)} all-gather(bf16[16,512]{1,0:T(8,128)(2,1)S(1)} %convert_element_type.312), channel_id=1, replica_groups=mesh['batch'=8,'head'=4] {'batch','head'}, dimensions={0}, use_global_device_ids=true | all-gather | bytes 540672 | tf_op jit(solution)/shard_map/all_gather | solution.py:281
  470.6 39.4 %all_gather.25 = bf16[2048,128]{1,0:T(8,128)(2,1)S(1)} all-gather(bf16[64,128]{1,0:T(8,128)(2,1)S(1)} %convert_element_type.301), channel_id=1, replica_groups=mesh['batch'=8,'head'=4] {'batch','head'}, dimensions={0}, use_global_device_ids=true | all-gather | bytes 540672 | tf_op jit(solution)/shard_map/all_gather | solution.py:282
  513.3 1.9 copy-done
  516.5 2.5 add_convert_fusion
  519.0 3.6 all-to-all-start
  523.0 3.1 fusion.124
  527.1 2.3 fusion.166
  529.4 7.8 %all-to-all-done = bf16[16,128,256]{2,1,0:T(8,128)(2,1)S(1)} async-done(((bf16[16,128,256]{2,1,0:T(8,128)(2,1)}), bf16[16,128,256]{2,1,0:T(8,128)(2,1)S(1)}, u32[]{:S(2)}, u32[]{:S(2)}) %all-to-all-start) | async-done | bytes 1048608 | tf_op jit(solution)/shard_map/all_to_all | solution.py:307
  540.9 2.5 multiply_reduce_fusion.15
  555.1 1.9 fusion.127
  558.3 1.9 multiply_convert_fusion.1
  560.2 1.8 fusion.122
  568.3 2.1 multiply_reduce_fusion.7
  570.4 2.1 convolution_bitcast_fusion.8
  572.5 1.9 multiply_reduce_fusion.5
  588.8 1.9 multiply_reduce_fusion.9
  597.4 37.2 %psum.31 = f32[6,128]{1,0:T(8,128)S(1)} all-reduce(f32[6,128]{1,0:T(8,128)S(1)} %reshape.333), channel_id=1, replica_groups=mesh['batch'=8,'head'=4] {'batch','head'}, use_global_device_ids=true, to_apply=%region_43.44 | all-reduce | flops 768 | bytes 6144 | tf_op jit(solution)/shard_map/psum | solution.py:349
  636.0 2.1 convolution_add_fusion
  638.1 92.7 %all-reduce.3.cloned.1.call-done = (f32[1024,128]{1,0:T(8,128)}, f32[512,512]{1,0:T(8,128)}, f32[2048,128]{1,0:T(8,128)}) async-done(((f32[1024,128]{1,0:T(8,128)}, f32[512,512]{1,0:T(8,128)}, f32[2048,128]{1,0:T(8,128)}), (f32[1024,128]{1,0:T(8,128)}, f32[512,512]{1,0:T(8,128)}, f32[2048,128]{1,0:T(8,128)})) %all-reduce.3.cloned.1.call-update) | async-done | bytes 2621456 | tf_op jit(solution)/shard_map/psum | solution.py:349
  730.7 2.1 multiply_reduce_fusion.2
  732.8 2.1 multiply_reduce_fusion.3
  734.9 1.8 multiply_reduce_fusion.4
  (273 shorter events, 70.1 us)
Async XLA Ops:
  7.2 40.1 %all-gather.5.cloned.1.call-start = ((), (), s32[]{:S(2)}) async-start(), calls=%async_computation.6 | async-start | bytes 5242880 | tf_op jit(solution)/shard_map/all_gather | solution.py:92
  7.9 107.2 %reduce-scatter.5.cloned.1.call-start = ((), (), s32[]{:S(2)}) async-start(), calls=%async_computation.7 | async-start | bytes 5242880 | tf_op jit(solution)/shard_map/reduce_scatter | solution.py:94
  67.2 47.9 %copy-start.4 = (bf16[16,128,256]{2,1,0:T(8,128)(2,1)S(1)}, bf16[16,128,256]{2,1,0:T(8,128)(2,1)}, u32[]{:S(2)}) copy-start(bf16[16,128,256]{2,1,0:T(8,128)(2,1)} %param.21) | copy-start | bytes 3145732
  70.5 82.5 %all-gather.7.cloned.1.call-start = ((), (), s32[]{:S(2)}) async-start(), calls=%async_computation.8 | async-start | bytes 5242880 | tf_op jit(solution)/shard_map/all_gather | solution.py:92
  117.8 96.4 %reduce-scatter.7.cloned.1.call-start = ((), (), s32[]{:S(2)}) async-start(), calls=%async_computation.9 | async-start | bytes 5242880 | tf_op jit(solution)/shard_map/reduce_scatter | solution.py:94
  169.5 44.7 %copy-start.3 = (bf16[16,128,256]{2,1,0:T(8,128)(2,1)S(1)}, bf16[16,128,256]{2,1,0:T(8,128)(2,1)}, u32[]{:S(2)}) copy-start(bf16[16,128,256]{2,1,0:T(8,128)(2,1)} %add_convert_fusion.3) | copy-start | bytes 3145732
  169.5 82.5 %all-gather.9.cloned.1.call-start = ((), (), s32[]{:S(2)}) async-start(), calls=%async_computation.10 | async-start | bytes 5242880 | tf_op jit(solution)/shard_map/all_gather | solution.py:92
  216.8 103.0 %reduce-scatter.9.cloned.1.call-start = ((), (), s32[]{:S(2)}) async-start(), calls=%async_computation.11 | async-start | bytes 5242880 | tf_op jit(solution)/shard_map/reduce_scatter | solution.py:94
  275.2 82.7 %all-gather.11.cloned.1.call-start = ((), (), s32[]{:S(2)}) async-start(), calls=%async_computation.12 | async-start | bytes 5242880 | tf_op jit(solution)/shard_map/all_gather | solution.py:92
  322.7 193.8 %reduce-scatter.11.cloned.1.call-start = ((), (), s32[]{:S(2)}) async-start(), calls=%async_computation.13 | async-start | bytes 5242880 | tf_op jit(solution)/shard_map/reduce_scatter | solution.py:94
  374.4 54.7 %copy-start.35 = (f32[16,512]{1,0:T(8,128)S(1)}, f32[16,512]{1,0:T(8,128)}, u32[]{:S(2)}) copy-start(f32[16,512]{1,0:T(8,128)} %param.33) | copy-start | bytes 98308
  374.5 54.7 %copy-start.34 = (f32[64,128]{1,0:T(8,128)S(1)}, f32[64,128]{1,0:T(8,128)}, u32[]{:S(2)}) copy-start(f32[64,128]{1,0:T(8,128)} %param.36) | copy-start | bytes 98308
  374.5 135.7 %copy-start.23 = (bf16[4,128,128]{2,1,0:T(8,128)(2,1)S(1)}, bf16[4,128,128]{2,1,0:T(8,128)(2,1)}, u32[]{:S(2)}) copy-start(bf16[4,128,128]{2,1,0:T(8,128)(2,1)} %param.28) | copy-start | bytes 393220
  376.6 135.3 %copy-start.58 = (f32[1,128]{1,0:T(1,128)}, f32[1,128]{1,0:T(1,128)S(1)}, u32[]{:S(2)}) copy-start(f32[1,128]{1,0:T(1,128)S(1)} %get-tuple-element.75) | copy-start | bytes 1540
  376.6 135.7 %copy-start.63 = (f32[128]{0:T(128)}, f32[128]{0:T(128)S(1)}, u32[]{:S(2)}) copy-start(f32[128]{0:T(128)S(1)} %get-tuple-element.74) | copy-start | bytes 1540
  377.1 135.2 %copy-start.60 = (f32[128]{0:T(128)}, f32[128]{0:T(128)S(1)}, u32[]{:S(2)}) copy-start(f32[128]{0:T(128)S(1)} %get-tuple-element.73) | copy-start | bytes 1540
  377.3 132.8 %all-to-all-start.1 = ((bf16[16,128,256]{2,1,0:T(8,128)(2,1)}), bf16[16,128,256]{2,1,0:T(8,128)(2,1)S(1)}, u32[]{:S(2)}, u32[]{:S(2)}) async-start(bf16[16,128,256]{2,1,0:T(8,128)(2,1)} %add_convert_fusion.2), calls=%async_computation.5 | async-start | bytes 2097152 | tf_op jit(solution)/shard_map/all_to_all | solution.py:307
  429.2 96.9 %copy-start.13 = (bf16[1024,128]{1,0:T(8,128)(2,1)}, bf16[1024,128]{1,0:T(8,128)(2,1)S(1)}, u32[]{:S(2)}) copy-start(bf16[1024,128]{1,0:T(8,128)(2,1)S(1)} %all_gather.26) | copy-start | bytes 786436
  429.9 83.4 %copy-start.27 = (bf16[384,128]{1,0:T(8,128)(2,1)}, bf16[384,128]{1,0:T(8,128)(2,1)S(1)}, u32[]{:S(2)}) copy-start(bf16[384,128]{1,0:T(8,128)(2,1)S(1)} %get-tuple-element.65) | copy-start | bytes 294916
  512.3 10.6 %copy-start.8 = (bf16[3,4,128,128]{2,3,0,1:T(8,128)(2,1)}, bf16[3,4,128,128]{2,3,0,1:T(8,128)(2,1)S(1)}, u32[]{:S(2)}) copy-start(bf16[3,4,128,128]{2,3,0,1:T(8,128)(2,1)S(1)} %fusion.114) | copy-start | bytes 1179652
  519.0 8.0 %copy-start.50 = (f32[128]{0:T(128)S(1)}, f32[128]{0:T(128)}, u32[]{:S(2)}) copy-start(f32[128]{0:T(128)} %get-tuple-element.72) | copy-start | bytes 1540
  519.0 18.1 %all-to-all-start = ((bf16[16,128,256]{2,1,0:T(8,128)(2,1)}), bf16[16,128,256]{2,1,0:T(8,128)(2,1)S(1)}, u32[]{:S(2)}, u32[]{:S(2)}) async-start(bf16[16,128,256]{2,1,0:T(8,128)(2,1)} %add_convert_fusion), calls=%async_computation.4 | async-start | bytes 2097152 | tf_op jit(solution)/shard_map/all_to_all | solution.py:307
  522.7 208.0 %all-reduce.3.cloned.1.call-start = ((), (), s32[]{:S(2)}) async-start(), calls=%async_computation.14 | async-start | bytes 5242880 | tf_op jit(solution)/shard_map/psum | solution.py:349
  526.4 14.4 %copy-start.65 = (f32[1,128]{1,0:T(1,128)S(1)}, f32[1,128]{1,0:T(1,128)}, u32[]{:S(2)}) copy-start(f32[1,128]{1,0:T(1,128)} %get-tuple-element.53) | copy-start | bytes 1540
  526.4 14.4 %copy-start.70 = (f32[128]{0:T(128)S(1)}, f32[128]{0:T(128)}, u32[]{:S(2)}) copy-start(f32[128]{0:T(128)} %get-tuple-element.52) | copy-start | bytes 1540
  527.0 16.3 %copy-start.38 = (f32[4,128]{1,0:T(4,128)}, f32[4,128]{1,0:T(4,128)S(1)}, u32[]{:S(2)}) copy-start(f32[4,128]{1,0:T(4,128)S(1)} %get-tuple-element.79) | copy-start | bytes 6148
  527.0 16.9 %copy-start.29 = (bf16[384,128]{1,0:T(8,128)(2,1)S(1)}, bf16[384,128]{1,0:T(8,128)(2,1)}, u32[]{:S(2)}) copy-start(bf16[384,128]{1,0:T(8,128)(2,1)} %get-tuple-element.64) | copy-start | bytes 294916
  527.0 16.9 %copy-start.62 = (f32[128]{0:T(128)S(1)}, f32[128]{0:T(128)}, u32[]{:S(2)}) copy-start(f32[128]{0:T(128)} %get-tuple-element.71) | copy-start | bytes 1540
  568.3 6.0 copy-start.66
  568.3 6.5 copy-start.17
  568.3 6.5 copy-start.71
  570.4 5.7 copy-start.12
  585.2 6.9 copy-start.14
  585.2 6.8 copy-start.24
  585.2 6.8 copy-start.55
  586.4 6.0 copy-start.59
  594.1 41.1 %copy-start.64 = (f32[128]{0:T(128)S(1)}, f32[128]{0:T(128)}, u32[]{:S(2)}) copy-start(f32[128]{0:T(128)} %copy-done.63) | copy-start | bytes 1540
  595.2 40.8 %copy-start.16 = (f32[4,128,512]{2,1,0:T(8,128)S(1)}, f32[4,128,512]{2,1,0:T(8,128)}, u32[]{:S(2)}) copy-start(f32[4,128,512]{2,1,0:T(8,128)} %copy-done.15) | copy-start | bytes 3145732
  597.2 142.2 %copy-start.54 = (f32[6,128]{1,0:T(8,128)S(1)}, f32[6,128]{1,0:T(8,128)}, u32[]{:S(2)}) copy-start(f32[6,128]{1,0:T(8,128)} %param.39) | copy-start | bytes 9220
  597.2 142.2 %copy-start.68 = (f32[6,128]{1,0:T(8,128)S(1)}, f32[6,128]{1,0:T(8,128)}, u32[]{:S(2)}) copy-start(f32[6,128]{1,0:T(8,128)} %param.40) | copy-start | bytes 9220
  597.2 142.2 %copy-start.69 = (f32[6,128]{1,0:T(8,128)S(1)}, f32[6,128]{1,0:T(8,128)}, u32[]{:S(2)}) copy-start(f32[6,128]{1,0:T(8,128)} %param.41) | copy-start | bytes 9220
  597.2 142.9 %copy-start.41 = (f32[64,128]{1,0:T(8,128)S(1)}, f32[64,128]{1,0:T(8,128)}, u32[]{:S(2)}) copy-start(f32[64,128]{1,0:T(8,128)} %param.37) | copy-start | bytes 98308
  597.2 142.9 %copy-start.42 = (f32[64,128]{1,0:T(8,128)S(1)}, f32[64,128]{1,0:T(8,128)}, u32[]{:S(2)}) copy-start(f32[64,128]{1,0:T(8,128)} %param.38) | copy-start | bytes 98308
  597.2 144.3 %copy-start.36 = (f32[16,512]{1,0:T(8,128)S(1)}, f32[16,512]{1,0:T(8,128)}, u32[]{:S(2)}) copy-start(f32[16,512]{1,0:T(8,128)} %param.33) | copy-start | bytes 98308
  597.2 144.3 %copy-start.43 = (f32[16,512]{1,0:T(8,128)S(1)}, f32[16,512]{1,0:T(8,128)}, u32[]{:S(2)}) copy-start(f32[16,512]{1,0:T(8,128)} %param.34) | copy-start | bytes 98308
  597.2 144.2 %copy-start.44 = (f32[16,512]{1,0:T(8,128)S(1)}, f32[16,512]{1,0:T(8,128)}, u32[]{:S(2)}) copy-start(f32[16,512]{1,0:T(8,128)} %param.35) | copy-start | bytes 98308
  597.2 145.7 %copy-start.48 = (f32[32,128]{1,0:T(8,128)S(1)}, f32[32,128]{1,0:T(8,128)}, u32[]{:S(2)}) copy-start(f32[32,128]{1,0:T(8,128)} %param.31) | copy-start | bytes 49156
  597.2 145.6 %copy-start.49 = (f32[32,128]{1,0:T(8,128)S(1)}, f32[32,128]{1,0:T(8,128)}, u32[]{:S(2)}) copy-start(f32[32,128]{1,0:T(8,128)} %param.32) | copy-start | bytes 49156
  (40 other events, 116.5 us)
Sparse Core Ops, SparseCore 0:
  9.6 37.7 all-gather.4
  70.6 44.4 reduce-scatter.4
  117.9 35.0 all-gather.6
  169.7 44.5 reduce-scatter.6
  217.0 35.0 all-gather.8
  275.3 44.4 reduce-scatter.8
  322.8 35.0 all-gather.10
  374.6 46.9 reduce-scatter.10
  597.4 133.2 all-reduce.2
where the time goes:
time: 759 us; the launch traced here: 752 us
  waiting for transfers between devices  377 us (50%)
  blocking collectives  166 us (22%)
  matrix products  108 us (14%)
  other arithmetic  52.6 us (7%)
  local copies, waits for them, and re-layouts  21.5 us (3%)
  between operations  18.9 us (2%)
  starting transfers between devices  8.47 us (1%)
    all_gather x4, waiting for transfers between devices, head_sublayer(): whole = lax.all_gather(hidden, 'head', axis=2, tiled=True)  142 us
    reduce_scatter x4, waiting for transfers between devices, head_sublayer(): lax.psum_scatter(work(normed).astype(jnp.bfloat16), 'head', scatter_dimen...  134 us
    psum x1, waiting for transfers between devices, shards(): lax.psum((grad_attend, grad_feed, grad_down, grad_gains), ('batch', 'head'))  92.7 us
    all_gather x1, blocking collectives, shards(): lax.all_gather(attend_master.astype(jnp.bfloat16), ('batch', 'head'), axi...  48.3 us
    all_gather x1, blocking collectives, shards(): lax.all_gather(feed_master.astype(jnp.bfloat16), ('batch', 'head'), axis=...  40.7 us
    all_gather x1, blocking collectives, shards(): lax.all_gather(down_master.astype(jnp.bfloat16), ('batch', 'head'), axis=...  39.4 us
    psum x1, blocking collectives, shards(): lax.psum((grad_attend, grad_feed, grad_down, grad_gains), ('batch', 'head'))  37.2 us
    dot_general x2, matrix products, feed_part(): jnp.einsum('rtf,fd->rtd', inner, w_reduce, preferred_element_type=jnp.flo...  26.9 us
  transfers between devices with their start and end apart: 11, of which 9 were waited for; matrix products, arithmetic and copies ran while one was open for 3% of the time, Pallas kernels for 0%

commit v1 on v0

v1 whole, which is shorter than its diff:
```python
from functools import partial

import jax
import jax.numpy as jnp
from jax import lax
from jax.experimental import pallas as pl
from jax.experimental.pallas import tpu as pltpu
from jax.sharding import PartitionSpec as P

D = 1024
HEAD_DIM = 64
S = 128
SIDE_HD = 8
SF = 512
L = 2
ROW = 128
STEP = 10


NORM_EPS = 1e-06
THRESHOLD = 1.0
BETA_ONE = 0.9
BETA_TWO = 0.999
ADAM_EPS = 1e-08
RATE_MATRIX = 0.12
RATE_SMALL = 0.5
WEIGHT_DECAY = 0.01
MASKED = -1e30

BF = jnp.bfloat16
F32 = jnp.float32
BLK = 256
PLACES = 32
MIB = 2**20

VM = pl.BlockSpec(memory_space=pltpu.VMEM)
SM = pl.BlockSpec(memory_space=pltpu.SMEM)
HB = pl.BlockSpec(memory_space=pltpu.HBM)


def shape_of(dims, kind):
    return jax.ShapeDtypeStruct(dims, kind)


def params(mib):
    return pltpu.CompilerParams(vmem_limit_bytes=mib * MIB)


def cost(micros):
    return pl.CostEstimate(flops=int(micros * 4e9), bytes_accessed=0, transcendentals=0)


def gelu(values):
    squared = values * values
    half = 0.5 * values
    bent = jnp.tanh(values * (0.7978845608028654 + 0.7978845608028654 * 0.044715 * squared))
    return half + half * bent


class Fetch:
    def __init__(self, sems):
        self.sems, self.items = sems, []

    def start(self, source, target):
        item = pltpu.make_async_copy(source, target, self.sems.at[len(self.items)])
        self.items.append(item)
        item.start()
        return item


def nn(a, b):
    return lax.dot_general(a, b, (((1,), (0,)), ((), ())), preferred_element_type=F32)


def nt(a, b):
    return lax.dot_general(a, b, (((1,), (1,)), ((), ())), preferred_element_type=F32)


def norm_scale(values):
    return lax.rsqrt(jnp.mean(values * values, axis=-1, keepdims=True) + NORM_EPS)


def root_norm(values, gains):
    return values * norm_scale(values) * gains


def segments(lengths):
    sent_ends = jnp.cumsum(lengths, axis=-1)
    kept_flag = sent_ends <= ROW
    places = jnp.arange(ROW, dtype=jnp.int32)
    labels = jnp.sum(
        (kept_flag[:, None, :] & (sent_ends[:, None, :] <= places[None, :, None])).astype(
            jnp.int32
        ),
        axis=-1,
    )
    filled = jnp.sum(jnp.where(kept_flag, lengths, 0), axis=-1)
    real_tok = (places[None, :] < filled[:, None]).astype(jnp.float32)
    return (labels[:, :, None] == labels[:, None, :], real_tok)


def side_by_side(rows2):
    return jnp.concatenate([rows2[:ROW], rows2[ROW:]], axis=1)


def block_diagonal(rows2):
    blank = jnp.zeros((ROW, ROW), rows2.dtype)
    top = jnp.concatenate([rows2[:ROW], blank], axis=1)
    low = jnp.concatenate([blank, rows2[ROW:]], axis=1)
    return jnp.concatenate([top, low], axis=0)


def head_masks(head_dim, first):
    lanes = lax.broadcasted_iota(jnp.int32, (ROW, 2 * ROW), 1) % ROW // head_dim
    return (lanes == first, lanes == first + 1)


def stack_heads(wide, masks):
    blank = jnp.zeros_like(wide)
    return jnp.concatenate(
        [jnp.where(masks[0], wide, blank), jnp.where(masks[1], wide, blank)], axis=0
    )


def pair_shares(key_stack, query_diag, bias, scale):
    scores = nt(key_stack, query_diag)
    if scale is not None:
        scores = scores * scale
    scores = scores.reshape(2, ROW, 2 * ROW) + bias[None]
    highest = jnp.max(scores, axis=1, keepdims=True)
    weights = jnp.exp(scores - highest)
    return weights * (1.0 / jnp.sum(weights, axis=1, keepdims=True))


def head_rows(flipped, count):
    rows = lax.broadcasted_iota(jnp.int32, flipped.shape, 0)
    blank = jnp.zeros_like(flipped)
    return jnp.concatenate(
        [jnp.where(rows < count, flipped, blank), jnp.where(rows >= count, flipped, blank)], axis=1
    )


def unrolled(count, step, width=2):
    def some(turn, carry):
        for at in range(width):
            step(turn * width + at)
        return carry

    lax.fori_loop(0, count // width, some, 0)


def flip(values):
    return values.astype(F32).T


def backbone_heads(proj, bias_ref, context_ref):
    masks = head_masks(HEAD_DIM, 0)
    for pair in range(proj.shape[1] // (2 * ROW)):
        rows = slice(pair * 2 * ROW, (pair + 1) * 2 * ROW)
        bias = bias_ref[pair]
        for lane_at in range(proj.shape[2] // ROW):
            lanes = slice(lane_at * ROW, (lane_at + 1) * ROW)
            queries = proj[0, rows, lanes] * jnp.asarray(HEAD_DIM**-0.5, BF)
            keys = proj[1, rows, lanes]
            values = proj[2, rows, lanes]
            shares = pair_shares(
                stack_heads(side_by_side(keys), masks), block_diagonal(queries), bias, None
            )
            shares = shares.astype(BF).reshape(2 * ROW, 2 * ROW)
            for at in range(2):
                flipped = flip(values[at * ROW : (at + 1) * ROW]).astype(BF)
                out = nn(head_rows(flipped, HEAD_DIM), shares[:, at * ROW : (at + 1) * ROW])
                start = pair * 2 * ROW + at * ROW
                context_ref[start : start + ROW, lanes] = out.T.astype(BF)


def assemble_kernel(place, own, near, far, far_near, gains, hidden_ref, normed_ref, other_ref):
    rows = own.shape[0] // 2
    whole = (hidden_ref, other_ref)
    for core, target in enumerate(whole):
        mine = pl.ds((place[2] ^ core) * rows, rows)
        for step, piece in enumerate((own, near, far, far_near)):
            spot = pl.multiple_of((place[0] ^ step) * BLK, BLK)
            target[:, pl.ds(spot, BLK)] = piece[mine].reshape(rows * ROW, BLK)
    for source, target in zip(whole, (normed_ref, other_ref)):
        target[...] = root_norm(source[...].astype(F32), gains[0, 0:1]).astype(BF)


def attend_kernel(layer, normed, weights, bias, context, proj, held, sems):
    fetch = Fetch(sems)
    waits = [fetch.start(weights.at[layer, at], held.at[at]) for at in range(3)]
    for at in range(3):
        waits[at].wait()
        proj[at] = nn(normed[...], held[at]).astype(BF)
    backbone_heads(proj, bias, context)


def attend_far_kernel(layer, place, normed, bias, context_own, out, *rest):
    parts, (total, proj, context, turned, held, sems) = rest[:4], rest[4:]
    fetch = Fetch(sems)
    wait = fetch.start(out.at[layer], held)
    spots = [pl.ds(pl.multiple_of((place[1] ^ step) * BLK, BLK), BLK) for step in range(4)]
    for step, spot in enumerate(spots):
        turned[:, step * BLK : (step + 1) * BLK] = normed[:, spot]
    for at in range(3):
        weights = jnp.concatenate([part[at] for part in parts], axis=0)
        proj[at] = nn(turned[...], weights).astype(BF)
    backbone_heads(proj, bias, context)
    wait.wait()
    both = jnp.concatenate([context_own[...], context[...]], axis=1)
    for step, spot in enumerate(spots):
        weights = jnp.concatenate([held[:, spot], parts[step][3]], axis=0)
        total[:, spot] = nn(both, weights).astype(total.dtype)


def finish_kernel(gain_at, hidden, total, came, gains, *outs):
    value = hidden[...].astype(F32) + (total[...] + came[...].astype(F32))
    value = value.astype(BF)
    outs[0][...] = value
    if gain_at is not None:
        layer, at = gain_at
        outs[1][...] = root_norm(value.astype(F32), gains[layer, at : at + 1]).astype(BF)


def feed_kernel(layer, normed, expand, reduce, total_ref, wide, tall, sems):
    fetch = Fetch(sems)
    waits = []
    for at in range(expand.shape[2] // (2 * BLK)):
        units = pl.ds(at * 2 * BLK, 2 * BLK)
        waits.append(
            (
                fetch.start(expand.at[layer, :, units], wide.at[at]),
                fetch.start(reduce.at[layer, units, :], tall.at[at]),
            )
        )
    for at, (expand_wait, reduce_wait) in enumerate(waits):
        expand_wait.wait()
        inner = gelu(nn(normed[...], wide[at])).astype(BF)
        reduce_wait.wait()
        term = nn(inner, tall[at])
        if at == 0:
            total_ref[...] = term
        else:
            total_ref[...] += term


def feed_far_kernel(count, sets, *refs):
    normed, totals = refs[:sets], refs[sets : 2 * sets]
    parts, outs = refs[2 * sets : 2 * sets + count], refs[2 * sets + count :]
    for values, total, out in zip(normed, totals, outs):
        inners = [gelu(nn(values[...], part[0:4].reshape(D, BLK))).astype(BF) for part in parts]
        inner = jnp.concatenate(inners, axis=1)
        for at in range(4):
            weights = jnp.concatenate([part[4 + at] for part in parts], axis=0)
            columns = slice(at * BLK, (at + 1) * BLK)
            out[:, columns] = (total[:, columns] + nn(inner, weights)).astype(out.dtype)


def pack_first_kernel(place, hidden, attend, output, chip_far, chip_own, attend_part, sems):
    fetch = Fetch(sems)
    spot = pl.ds(pl.multiple_of(place[1] * BLK, BLK), BLK)
    for at in range(3):
        fetch.start(attend.at[0, at, spot, :], attend_part.at[at])
    fetch.start(output.at[0, :, spot], attend_part.at[3])
    rows = chip_own.shape[0]
    fetch.start(hidden.at[pl.ds((1 - place[3]) * rows, rows)], chip_far)
    fetch.start(hidden.at[pl.ds(place[3] * rows, rows)], chip_own)
    for item in fetch.items:
        item.wait()


def pack_first(place, hidden, attend, output):
    half = (hidden.shape[0] // 2,) + hidden.shape[1:]
    return pl.pallas_call(
        pack_first_kernel,
        out_shape=[shape_of(half, BF)] * 2 + [shape_of((4, BLK, BLK), BF)],
        in_specs=[SM] + [HB] * 3,
        out_specs=[VM] * 3,
        scratch_shapes=[pltpu.SemaphoreType.DMA((6,))],
        compiler_params=params(57),
        cost_estimate=cost(1.0),
    )(place, hidden, attend, output)


def pack_kernel(place, attend, output, expand, reduce, attend_part, *rest):
    feed_targets, sems = rest[:-1], rest[-1]
    fetch = Fetch(sems)
    spot = pl.ds(pl.multiple_of(place[1] * BLK, BLK), BLK)
    last = pl.ds(pl.multiple_of((place[1] ^ 3) * BLK, BLK), BLK)
    for layer, units, target in zip((0, 1, 1), (spot, spot, last), feed_targets):
        for at in range(4):
            rows = pl.ds(at * BLK, BLK)
            fetch.start(expand.at[layer, rows, units], target.at[at])
            fetch.start(reduce.at[layer, units, rows], target.at[4 + at])
    for at in range(3):
        fetch.start(attend.at[1, at, spot, :], attend_part.at[at])
    fetch.start(output.at[1, :, spot], attend_part.at[3])
    for item in fetch.items:
        item.wait()


def pack(place, attend, output, expand, reduce):
    return pl.pallas_call(
        pack_kernel,
        out_shape=[shape_of((4, BLK, BLK), BF)] + [shape_of((8, BLK, BLK), BF)] * 3,
        in_specs=[SM] + [HB] * 4,
        out_specs=[VM] * 4,
        scratch_shapes=[pltpu.SemaphoreType.DMA((28,))],
        compiler_params=params(57),
        cost_estimate=cost(2.0),
    )(place, attend, output, expand, reduce)


def prepare_kernel(lengths, place, cotangent, *rest):
    masters, (bias_ref, other_ref, seed_ref, *packed) = rest[:3], rest[3:]
    rows = cotangent.shape[0] // ROW
    deep = lax.broadcasted_iota(jnp.int32, (ROW, ROW), 0)
    across = lax.broadcasted_iota(jnp.int32, (ROW, ROW), 1)
    for row in range(2 * rows):
        core, row = row // rows, row % rows
        end = jnp.int32(0)
        filled = jnp.int32(0)
        deep_label = jnp.zeros((ROW, ROW), jnp.int32)
        across_label = jnp.zeros((ROW, ROW), jnp.int32)
        for slot in range(lengths.shape[1]):
            length = lengths[(place[0] ^ core) * rows + row, slot]
            end = end + length
            kept = end <= ROW
            filled = filled + jnp.where(kept, length, 0)
            start = jnp.where(kept, end, ROW)
            deep_label += (deep >= start).astype(jnp.int32)
            across_label += (across >= start).astype(jnp.int32)
        pair, at = row // 2, row % 2
        target = other_ref if core else bias_ref
        target[pair, :, at * ROW : (at + 1) * ROW] = jnp.where(
            deep_label == across_label, 0.0, MASKED
        )
        if core:
            continue
        spot = slice(row * ROW, (row + 1) * ROW)
        seed_ref[spot] = jnp.where(deep < filled, cotangent[spot], 0.0)
    if packed:
        base = 0
        for master in masters:
            height, width = master.shape
            for column in range(width // S):
                packed[0][0, base : base + height] = master[:, column * S : (column + 1) * S].astype(BF)
                base += height


def prepare(lengths, place, cotangent, masters, packed):
    tokens = cotangent.shape[0]
    shapes = [shape_of((tokens // ROW // 2, ROW, 2 * ROW), F32)] * 2 + [shape_of((tokens, S), F32)]
    if packed:
        shapes.append(shape_of((1, sum(master.size for master in masters) // S, S), BF))
    return pl.pallas_call(
        prepare_kernel,
        out_shape=shapes,
        in_specs=[SM, SM] + [VM] * 4,
        out_specs=[VM] * len(shapes),
        compiler_params=params(8),
        cost_estimate=cost(1.5),
    )(lengths, place, cotangent, *masters)


SAVED = (
    ("tapped", F32),
    ("mixed", F32),
    ("middle", F32),
    ("queries", BF),
    ("keys", BF),
    ("values", BF),
    ("context", BF),
)


def gathered_at(device):
    order = (1, 2, 3, 4, 0)
    return sum((device >> bit & 1) << at for at, bit in enumerate(order))


def matrix_loader(place, whole, places):
    heights = (L * 4 * S // places, L * 2 * S // places, L * D // places)
    feed_base = heights[0]
    down_base = feed_base + heights[1] * (SF // S)

    def rows(first, total, base, height):
        start = first // height
        return jnp.concatenate(
            [
                whole[gathered_at(start + step) ^ place[9], base : base + height]
                for step in range(total // height)
            ],
            axis=0,
        )

    def load(layer, mats, feeds, down=None):
        for at in range(4):
            mats[at] = rows((layer * 4 + at) * S, S, 0, heights[0])
        for at in range(2):
            for column in range(SF // S):
                feeds[at, :, column * S : (column + 1) * S] = rows(
                    (layer * 2 + at) * S, S, feed_base + column * heights[1], heights[1]
                )
        if down is not None:
            down[...] = rows(layer * D, D, down_base, heights[2])

    return load


def side_forward(tap_source, down, state, mats, feeds, smalls, bias_ref, saved, flips, result_ref):
    tokens = state.shape[0]
    gating = jax.nn.sigmoid(smalls[2:3])
    tapped = nn(tap_source, down)
    mixed = gating * tapped + (1.0 - gating) * state
    saved["tapped"][...] = tapped
    saved["mixed"][...] = mixed
    normed = (mixed * norm_scale(mixed) * smalls[0:1]).astype(BF)
    for at, name in enumerate(("queries", "keys", "values")):
        saved[name][...] = nn(normed, mats[at]).astype(BF)
    for at in range(tokens // ROW):
        flips[0, at] = flip(saved["values"][at * ROW : (at + 1) * ROW]).astype(BF)
    pairs = tokens // (2 * ROW)
    heads = S // SIDE_HD // 2

    def step(turn):
        pair, head = turn // heads, turn % heads
        rows = pl.ds(pl.multiple_of(pair * 2 * ROW, 2 * ROW), 2 * ROW)
        masks = head_masks(SIDE_HD, 2 * head)
        shares = pair_shares(
            stack_heads(side_by_side(saved["keys"][rows]), masks),
            block_diagonal(saved["queries"][rows]),
            bias_ref[pair],
            SIDE_HD**-0.5,
        )
        shares = shares.astype(BF).reshape(2 * ROW, 2 * ROW)
        spot = pl.ds(pl.multiple_of(head * 2 * SIDE_HD, 2 * SIDE_HD), 2 * SIDE_HD)
        for at in range(2):
            lhs = head_rows(flips[0, 2 * pair + at, spot], SIDE_HD)
            flips[1, 2 * pair + at, spot] = nn(lhs, shares[:, at * ROW : (at + 1) * ROW]).astype(
                BF
            )

    unrolled(pairs * heads, step)
    for at in range(tokens // ROW):
        saved["context"][at * ROW : (at + 1) * ROW] = flip(flips[1, at]).astype(BF)
    middle = mixed + nn(saved["context"][...], mats[3])
    saved["middle"][...] = middle
    normed_two = (middle * norm_scale(middle) * smalls[1:2]).astype(BF)
    active = gelu(nn(normed_two, feeds[0])).astype(BF)
    result_ref[...] = middle + nt(active, feeds[1])


def gelu_parts(inner):
    root = 0.7978845608028654
    squared = inner * inner
    bent = jnp.tanh(root * inner * (1.0 + 0.044715 * squared))
    half = 0.5 * (1.0 + bent)
    slope = half + 0.5 * inner * (1.0 - bent * bent) * (root * (1.0 + 3.0 * 0.044715 * squared))
    return (inner * half, slope)


def norm_back(values, scale, gains, grad_normed):
    weighted = grad_normed * gains
    grad_values = scale * weighted - values * scale**3 * jnp.mean(
        weighted * values, axis=-1, keepdims=True
    )
    return (grad_values, jnp.sum(grad_normed * values * scale, axis=0, keepdims=True))


def side_backward(tap_source, state, grad_out, mats, feeds, smalls, bias_ref, saved, work, put):
    flips, grads, grad_flips = work
    tokens = grad_out.shape[0]
    pairs = tokens // (2 * ROW)
    heads = S // SIDE_HD // 2
    middle = saved["middle"][...]
    second_scale = norm_scale(middle)
    normed_two = (middle * second_scale * smalls[1:2]).astype(BF)
    active, slope = gelu_parts(nn(normed_two, feeds[0]))
    grad_outer = grad_out.astype(BF)
    put("feed", 1, nn(flip(grad_outer).astype(BF), active.astype(BF)))
    grad_inner = (nn(grad_outer, feeds[1]) * slope).astype(BF)
    put("feed", 0, nn(flip(normed_two).astype(BF), grad_inner))
    grad_middle, grad_gain_two = norm_back(
        middle, second_scale, smalls[1:2], nt(grad_inner, feeds[0])
    )
    put("gain", 1, grad_gain_two)
    grad_middle = grad_middle + grad_out
    grad_branch = grad_middle.astype(BF)
    put("attend", 3, nn(flip(saved["context"][...]).astype(BF), grad_branch))
    grads[0] = nt(grad_branch, mats[3]).astype(BF).astype(F32)
    grads[1] = jnp.zeros_like(grads[1])
    grads[2] = jnp.zeros_like(grads[2])
    for at in range(tokens // ROW):
        flips[0, at] = flip(saved["keys"][at * ROW : (at + 1) * ROW]).astype(BF)

    def step(turn):
        pair, head = turn // heads, turn % heads
        rows = pl.ds(pl.multiple_of(pair * 2 * ROW, 2 * ROW), 2 * ROW)
        masks = head_masks(SIDE_HD, 2 * head)
        query_diag = block_diagonal(saved["queries"][rows])
        context_diag = block_diagonal(grads[0, rows].astype(BF))
        shares = pair_shares(
            stack_heads(side_by_side(saved["keys"][rows]), masks),
            query_diag,
            bias_ref[pair],
            SIDE_HD**-0.5,
        )
        grad_shares = nt(stack_heads(side_by_side(saved["values"][rows]), masks), context_diag)
        grad_shares = grad_shares.reshape(2, ROW, 2 * ROW)
        mean = jnp.sum(shares * grad_shares, axis=1, keepdims=True)
        grad_scores = (shares * (grad_shares - mean)).astype(BF).reshape(2 * ROW, 2 * ROW)
        shares = shares.astype(BF).reshape(2 * ROW, 2 * ROW)
        for slot, left, right in ((2, shares, context_diag), (1, grad_scores, query_diag)):
            whole = nn(left, right)
            blank = jnp.zeros((ROW, 2 * ROW), F32)
            picked = jnp.where(masks[0], whole[:ROW], blank) + jnp.where(
                masks[1], whole[ROW:], blank
            )
            first = pl.ds(pl.multiple_of(pair * 2 * ROW, 2 * ROW), ROW)
            second = pl.ds(pl.multiple_of(pair * 2 * ROW + ROW, ROW), ROW)
            grads[slot, first] += picked[:, :ROW]
            grads[slot, second] += picked[:, ROW:]
        spot = pl.ds(pl.multiple_of(head * 2 * SIDE_HD, 2 * SIDE_HD), 2 * SIDE_HD)
        for at in range(2):
            lhs = head_rows(flips[0, 2 * pair + at, spot], SIDE_HD)
            grad_flips[2 * pair + at, spot] = nn(lhs, grad_scores[:, at * ROW : (at + 1) * ROW])

    unrolled(pairs * heads, step)
    for at in range(tokens // ROW):
        grads[0, at * ROW : (at + 1) * ROW] = grad_flips[at].T
    root = SIDE_HD**-0.5
    mixed = saved["mixed"][...]
    first_scale = norm_scale(mixed)
    normed_flip = flip((mixed * first_scale * smalls[0:1]).astype(BF)).astype(BF)
    grad_normed = None
    for at, factor in enumerate((root, root, None)):
        grad = grads[at] if factor is None else grads[at] * factor
        grad = grad.astype(BF)
        put("attend", at, nn(normed_flip, grad))
        term = nt(grad, mats[at])
        grad_normed = term if grad_normed is None else grad_normed + term
    grad_mixed, grad_gain_one = norm_back(mixed, first_scale, smalls[0:1], grad_normed)
    put("gain", 0, grad_gain_one)
    grad_mixed = grad_mixed + grad_middle
    gating = jax.nn.sigmoid(smalls[2:3])
    grad_tap = (gating * grad_mixed).astype(BF)
    put(
        "gain",
        2,
        jnp.sum(grad_mixed * (saved["tapped"][...] - state), axis=0, keepdims=True)
        * gating
        * (1.0 - gating),
    )
    put("down", 0, nn(flip(grad_tap).astype(BF), tap_source).T)
    return (1.0 - gating) * grad_mixed


MATRICES = [
    pltpu.VMEM((4, S, S), BF),
    pltpu.VMEM((2, S, SF), BF),
    pltpu.VMEM((D, S), BF),
]


def side_first_kernel(place, tap_source, whole, state, smalls, bias, *rest):
    outs, (flips, mats, feeds, down) = rest[:-4], rest[-4:]
    matrix_loader(place, whole, PLACES)(0, mats, feeds, down)
    saved = {name: ref for (name, _), ref in zip(SAVED, outs)}
    side_forward(
        tap_source[...],
        down[...],
        state[...].astype(F32),
        mats,
        feeds,
        smalls[0:3],
        bias,
        saved,
        flips,
        outs[-1],
    )


def side_first(place, tap_source, whole, state, smalls, bias):
    tokens = state.shape[0]
    return pl.pallas_call(
        side_first_kernel,
        out_shape=[shape_of((tokens, S), kind) for _, kind in SAVED]
        + [shape_of((tokens, S), F32)],
        in_specs=[SM] + [VM] * 5,
        out_specs=[VM] * (len(SAVED) + 1),
        scratch_shapes=[pltpu.VMEM((2, tokens // ROW, S, ROW), BF)] + MATRICES,
        compiler_params=params(16),
        cost_estimate=cost(8.0),
    )(place, tap_source, whole, state, smalls, bias)


def side_last_kernel(
    packed,
    place,
    tap_one,
    tap_two,
    whole_in,
    state_in,
    state,
    cotangent,
    smalls,
    bias,
    *rest,
):
    count = len(SAVED)
    saved_one = {name: ref for (name, _), ref in zip(SAVED, rest[:count])}
    rest = rest[count:]
    result_ref, grad_ref = rest[:2]
    outs = rest[2:4] if packed else rest[2:6]
    rest = rest[len(outs) + 2 :]
    saved_two = {name: ref for (name, _), ref in zip(SAVED, rest[:count])}
    flips, grads, grad_flips, mats, feeds, down = rest[count : count + 6]
    load = matrix_loader(place, whole_in, PLACES)
    load(1, mats, feeds, down)
    if packed:
        whole = rest[count + 6]
        places = whole.shape[0] * 2
        widths = (L * 4 * S // places, L * 2 * S // places, L * D // places)
        feed_base = widths[0]
        down_base = feed_base + widths[1] * (SF // S)
        gain_base = down_base + widths[2]
        whole[:, :, gain_base:, :] = jnp.zeros_like(whole[:, :, gain_base:, :])

    def put_at(layer, kind, at, value):
        if not packed:
            target = outs[("attend", "feed", "down", "gain").index(kind)]
            if kind == "gain":
                target[3 * layer + at : 3 * layer + at + 1] = value
            else:
                first = {"attend": (layer * 4 + at) * S, "feed": (layer * 2 + at) * S}.get(
                    kind, layer * D
                )
                target[first : first + value.shape[0]] = value
            return
        if kind == "gain":
            spot = gain_base + 3 * layer + at
            whole[:, :, spot : spot + 1, :] = jnp.broadcast_to(
                value[None, None], whole.shape[:2] + (1, S)
            )
            return
        width = widths[("attend", "feed", "down").index(kind)]
        half = value.shape[0] // width // 2
        if kind == "feed":
            start = (layer * 2 + at) * half
            for column in range(SF // S):
                spot = feed_base + column * width
                whole[start : start + half, :, spot : spot + width, :] = value[
                    :, column * S : (column + 1) * S
                ].reshape(half, 2, width, S)
        else:
            base = 0 if kind == "attend" else down_base
            start = (layer * 4 + at) * half if kind == "attend" else layer * half
            whole[start : start + half, :, base : base + width, :] = value.reshape(
                half, 2, width, S
            )

    work = (flips, grads, grad_flips)
    smalls_one, smalls_two = smalls[0:3], smalls[3:6]
    side_forward(
        tap_two[...],
        down[...],
        state[...],
        mats,
        feeds,
        smalls_two,
        bias,
        saved_two,
        flips,
        result_ref,
    )
    grad_now = side_backward(
        tap_two[...],
        state[...],
        cotangent[...],
        mats,
        feeds,
        smalls_two,
        bias,
        saved_two,
        work,
        partial(put_at, 1),
    )
    load(0, mats, feeds)
    grad_ref[...] = side_backward(
        tap_one[...],
        state_in[...].astype(F32),
        grad_now,
        mats,
        feeds,
        smalls_one,
        bias,
        saved_one,
        work,
        partial(put_at, 0),
    )
    if packed:
        mine = place[0] % 2
        outs[0][...] = whole[:, mine]
        outs[1][...] = whole[:, 1 - mine].astype(BF)


def side_last(places, place, tap_one, tap_two, whole, state_in, state, cotangent, smalls, bias, saved):
    tokens = state.shape[0]
    packed = places > 0
    shapes = [shape_of((tokens, S), F32)] * 2
    scratch = [pltpu.VMEM((tokens, S), kind) for _, kind in SAVED]
    scratch += [
        pltpu.VMEM((2, tokens // ROW, S, ROW), BF),
        pltpu.VMEM((3, tokens, S), F32),
        pltpu.VMEM((tokens // ROW, S, ROW), F32),
    ] + MATRICES
    if packed:
        height = (L * 4 * S + L * 2 * SF + L * D) // places + 16
        shapes += [
            shape_of((places // 2, height, S), F32),
            shape_of((places // 2, height, S), BF),
        ]
        scratch.append(pltpu.VMEM((places // 2, 2, height, S), F32))
    else:
        shapes += [
            shape_of((L * 4 * S, S), F32),
            shape_of((L * 2 * S, SF), F32),
            shape_of((L * D, S), F32),
            shape_of((L * 3, S), F32),
        ]
    return pl.pallas_call(
        partial(side_last_kernel, packed),
        out_shape=shapes,
        in_specs=[SM] + [VM] * (8 + len(SAVED)),
        out_specs=[VM] * len(shapes),
        scratch_shapes=scratch,
        compiler_params=params(32),
        cost_estimate=cost(30.0),
    )(place, tap_one, tap_two, whole, state_in, state, cotangent, smalls, bias, *saved)


def halve_kernel(bit, place, kept, came, keep_ref, send_ref):
    mine = place[2 + bit]
    half = keep_ref.shape[0]
    for at in range(half):
        for target, pick in ((keep_ref, mine), (send_ref, 1 - mine)):
            spot = 2 * at + pick
            target[at] = (kept[spot] + came[spot].astype(F32)).astype(target.dtype)


def halve(bit, place, kept, came):
    half = (kept.shape[0] // 2,) + kept.shape[1:]
    return pl.pallas_call(
        partial(halve_kernel, bit),
        out_shape=[shape_of(half, F32), shape_of(half, BF)],
        in_specs=[SM, VM, VM],
        out_specs=[VM, VM],
        compiler_params=params(16),
    )(place, kept, came)


def tally_kernel(place, kept, came, total_ref, squares_ref):
    total = kept[0] + came[0].astype(F32)
    total_ref[...] = total
    height = total.shape[0]
    squares = total * total
    matrix_part = jnp.sum(squares[: height - 16].reshape(-1, 8, S), axis=0)
    gain_part = jnp.sum(squares[height - 16 :].reshape(-1, 8, S), axis=0)
    squares_ref[...] = matrix_part + jnp.where(place[7] == 0, gain_part, jnp.zeros_like(gain_part))


def tally(place, kept, came):
    return pl.pallas_call(
        tally_kernel,
        out_shape=[shape_of(kept.shape[1:], F32), shape_of((8, S), F32)],
        in_specs=[SM, VM, VM],
        out_specs=[VM, VM],
        compiler_params=params(16),
    )(place, kept, came)


def adamw(master, moment, square, grad_now, clip, rate, decay):
    grad_now = grad_now * clip
    moment = BETA_ONE * moment + (1.0 - BETA_ONE) * grad_now
    square = BETA_TWO * square + (1.0 - BETA_TWO) * grad_now * grad_now
    first_hat = moment / (1.0 - BETA_ONE**STEP)
    second_hat = square / (1.0 - BETA_TWO**STEP)
    master = master - rate * (first_hat / (jnp.sqrt(second_hat) + ADAM_EPS) + decay * master)
    return (master, moment, square)


def update_kernel(total, squares, *refs):
    states, (norm_ref, *outs) = refs[:12], refs[12:]
    grad_norm = jnp.sqrt(jnp.sum(squares[...], keepdims=True))
    norm_ref[...] = grad_norm
    clip = jnp.minimum(1.0, THRESHOLD / grad_norm)
    base = 0
    for at, name in enumerate(("attend", "feed", "down", "gain")):
        master, moment, square = (ref[...] for ref in states[3 * at : 3 * at + 3])
        height, width = master.shape
        columns = []
        for _ in range(width // S):
            columns.append(total[base : base + height])
            base += height
        grad_now = columns[0] if len(columns) == 1 else jnp.concatenate(columns, axis=1)
        rate, decay = (RATE_SMALL, 0.0) if name == "gain" else (RATE_MATRIX, WEIGHT_DECAY)
        new = adamw(master, moment, square, grad_now, clip, rate, decay)
        for value, target in zip(new, outs[:3]):
            target[...] = value
        if name == "gain":
            outs = outs[3:]
        else:
            outs[3][...] = new[0].astype(BF)
            outs = outs[4:]


def update(total, squares, states):
    shapes = [shape_of((1, 1), F32)]
    for at in range(4):
        dims = states[3 * at].shape
        shapes += [shape_of(dims, F32)] * 3
        if at < 3:
            shapes.append(shape_of(dims, BF))
    return pl.pallas_call(
        update_kernel,
        out_shape=shapes,
        in_specs=[VM] * 14,
        out_specs=[VM] * len(shapes),
        compiler_params=params(16),
    )(total, squares, *states)


def swap(value, axis, bit):
    size = lax.axis_size(axis)
    return lax.ppermute(value, axis, [(at, at ^ bit) for at in range(size)])


def join(*values):
    return lax.optimization_barrier(values)


def backbone_rows(
    place,
    frozen_input,
    frozen_attend,
    frozen_output,
    frozen_expand,
    frozen_reduce,
    frozen_gains,
    biases,
    side_own,
    side_layer,
):
    rows = frozen_input.shape[0] // 4
    tokens = rows * ROW
    frozen = (frozen_attend, frozen_output, frozen_expand, frozen_reduce)
    chip_far, chip_own, attend_zero = pack_first(place, frozen_input, *frozen[:2])
    attend_one, feed_zero, feed_one, feed_far = pack(place, *frozen)

    def x(value):
        return swap(value, "head", 2)

    def y(value):
        return swap(value, "batch", 1)

    def z(value):
        return swap(value, "batch", 2)

    def near(value):
        return swap(value, "head", 1)

    def double(value, came):
        return jnp.concatenate([value, came], axis=0)

    wide = shape_of((tokens, D), BF)
    sums = shape_of((tokens, D), F32)

    def attend_own(layer, normed, bias):
        return pl.pallas_call(
            partial(attend_kernel, layer),
            out_shape=shape_of((tokens, BLK), BF),
            in_specs=[VM, HB, VM],
            out_specs=VM,
            scratch_shapes=[
                pltpu.VMEM((3, tokens, BLK), BF),
                pltpu.VMEM((3, D, BLK), BF),
                pltpu.SemaphoreType.DMA((3,)),
            ],
            compiler_params=params(16),
            cost_estimate=cost(3.0),
        )(normed, frozen_attend, bias)

    def attend_far(layer, normed, bias, context, kind, parts):
        return pl.pallas_call(
            partial(attend_far_kernel, layer),
            out_shape=shape_of((tokens, D), kind),
            in_specs=[SM] + [VM] * 3 + [HB] + [VM] * 4,
            out_specs=VM,
            scratch_shapes=[
                pltpu.VMEM((3, tokens, BLK), BF),
                pltpu.VMEM((tokens, BLK), BF),
                pltpu.VMEM((tokens, D), BF),
                pltpu.VMEM((BLK, D), BF),
                pltpu.SemaphoreType.DMA((1,)),
            ],
            compiler_params=params(16),
            cost_estimate=cost(4.0),
        )(place, normed, bias, context, frozen_output, *parts)

    def finish(gain_at, hidden, total, came):
        count = 1 if gain_at is None else 2
        return pl.pallas_call(
            partial(finish_kernel, gain_at),
            out_shape=[wide] * count,
            in_specs=[VM] * 4,
            out_specs=[VM] * count,
            compiler_params=params(12),
            cost_estimate=cost(1.0),
        )(hidden, total, came, frozen_gains)

    def feed_own(layer, normed):
        return pl.pallas_call(
            partial(feed_kernel, layer),
            out_shape=sums,
            in_specs=[VM] + [HB] * 2,
            out_specs=VM,
            scratch_shapes=[
                pltpu.VMEM((2, D, 2 * BLK), BF),
                pltpu.VMEM((2, 2 * BLK, D), BF),
                pltpu.SemaphoreType.DMA((4,)),
            ],
            compiler_params=params(16),
            cost_estimate=cost(3.0),
        )(normed, frozen_expand, frozen_reduce)

    def feed_far_units(normed, totals, parts, kind=F32):
        sets = len(normed)
        return pl.pallas_call(
            partial(feed_far_kernel, len(parts), sets),
            out_shape=[shape_of((tokens, D), kind)] * sets,
            in_specs=[VM] * (2 * sets + len(parts)),
            out_specs=[VM] * sets,
            compiler_params=params(16),
            cost_estimate=cost(1.0 * sets * len(parts)),
        )(*normed, *totals, *parts)

    a0x, near_own = x(attend_zero), near(chip_own)
    side = double(side_own, x(side_own))
    side = double(side, y(side))
    side = double(side, z(side))

    a0x, near_own, chip_far, side = join(a0x, near_own, chip_far, side)
    far, a0y, a0z = x(chip_far), y(a0x), z(a0x)
    side_came = swap(side, "batch", 4)

    far, a0y, a0z, feed_zero, side, side_came = join(far, a0y, a0z, feed_zero, side, side_came)
    far_near, f0x, a0w = near(far), x(feed_zero), y(a0z)
    side = double(side, side_came)
    hidden, normed, other = pl.pallas_call(
        assemble_kernel,
        out_shape=[wide] * 3,
        in_specs=[SM] + [VM] * 5,
        out_specs=[VM] * 3,
        compiler_params=params(16),
        cost_estimate=cost(2.0),
    )(place, chip_own, near_own, far, far_near, frozen_gains)
    context = attend_own(0, normed, biases[0])
    other_context = attend_own(0, other, biases[1])

    context, other_context, a0w, side = join(context, other_context, a0w, side)
    side = double(side, near(side))
    parts = (a0x, a0y, a0z, a0w)
    came = near(attend_far(0, other, biases[1], other_context, BF, parts))
    total = attend_far(0, normed, biases[0], context, F32, parts)
    mid, normed = finish((0, 1), hidden, total, came)

    mid, normed, f0x, attend_one, side = join(mid, normed, f0x, attend_one, side)
    other, a1x, f0y, f0z = near(normed), x(attend_one), y(f0x), z(f0x)
    total = feed_own(0, normed)
    other_total = feed_own(0, other)

    total, other_total, a1x, feed_one = join(total, other_total, a1x, feed_one)
    f1x = x(feed_one)
    f0y, f0z, a1x = join(f0y, f0z, a1x)
    f0w, a1y = z(f0y), y(a1x)
    total, other_total = feed_far_units((normed, other), (total, other_total), (f0x, f0y, f0z))

    total, other_total, f1x, feed_far = join(total, other_total, f1x, feed_far)
    f1w = x(feed_far)
    f0w, a1y, f1x, a1x = join(f0w, a1y, f1x, a1x)
    f1y, a1z = y(f1x), z(a1x)
    came = near(feed_far_units((other,), (other_total,), (f0w,), BF)[0])
    total = feed_far_units((normed,), (total,), (f0w,))[0]
    hidden, normed = finish((1, 0), mid, total, came)
    taps = [hidden]
    other = near(normed)
    context = attend_own(1, normed, biases[0])
    other_context = attend_own(1, other, biases[1])

    context, other_context, a1z, f1x = join(context, other_context, a1z, f1x)
    a1w, f1z = y(a1z), z(f1x)
    side_outs = side_layer(hidden, side)
    a1w, *side_outs = join(a1w, *side_outs)
    parts = (a1x, a1y, a1z, a1w)
    came = near(attend_far(1, other, biases[1], other_context, BF, parts))
    total = attend_far(1, normed, biases[0], context, F32, parts)
    mid, normed = finish((1, 1), hidden, total, came)
    other = near(normed)
    total = feed_own(1, normed)
    other_total = feed_own(1, other)
    total, other_total = feed_far_units((normed, other), (total, other_total), (f1x, f1y))
    total, other_total, f1w, f1z = join(total, other_total, f1w, f1z)
    came = near(feed_far_units((other,), (other_total,), (f1w, f1z), BF)[0])
    total = feed_far_units((normed,), (total,), (f1w, f1z))[0]
    taps.append(finish(None, mid, total, came)[0])
    return (taps, side, side_outs)


def split_attend(normed, w_attend, w_output, same_seg):
    col_count = w_attend.shape[2]
    projected = jnp.einsum(
        "rtd,jdc->jrtc", normed, w_attend, preferred_element_type=jnp.float32
    ).astype(jnp.bfloat16)
    head_shape = normed.shape[:2] + (col_count // HEAD_DIM, HEAD_DIM)
    queries = projected[0].reshape(head_shape)
    key_rows = projected[1].reshape(head_shape)
    value_rows = projected[2].reshape(head_shape)
    scores = jnp.einsum(
        "rqhc,rkhc->rhqk", queries, key_rows, preferred_element_type=jnp.float32
    ) * HEAD_DIM ** (-0.5)
    scores = jnp.where(same_seg[:, None], scores, MASKED)
    shares = jax.nn.softmax(scores, axis=-1).astype(jnp.bfloat16)
    context = jnp.einsum("rhqk,rkhc->rqhc", shares, value_rows, preferred_element_type=jnp.float32)
    context = context.astype(jnp.bfloat16).reshape(normed.shape[:2] + (col_count,))
    return jnp.einsum("rtc,cd->rtd", context, w_output, preferred_element_type=jnp.float32)


def split_feed(normed, w_expand, w_reduce):
    inner = jax.nn.gelu(
        jnp.einsum("rtd,df->rtf", normed, w_expand, preferred_element_type=jnp.float32)
    ).astype(jnp.bfloat16)
    return jnp.einsum("rtf,fd->rtd", inner, w_reduce, preferred_element_type=jnp.float32)


def split_sublayer(hidden, gains, work):
    whole = lax.all_gather(hidden, "head", axis=2, tiled=True)
    normed = root_norm(whole.astype(jnp.float32), gains).astype(jnp.bfloat16)
    summed = lax.psum_scatter(
        work(normed).astype(jnp.bfloat16), "head", scatter_dimension=2, tiled=True
    ).astype(jnp.float32)
    return (hidden.astype(jnp.float32) + summed).astype(jnp.bfloat16)


def backbone_split(
    frozen_input, frozen_attend, frozen_output, frozen_expand, frozen_reduce, frozen_gains, lengths
):
    taps = []
    same_all, _ = segments(lengths)
    hidden = frozen_input
    for layer in range(L):
        hidden = split_sublayer(
            hidden,
            frozen_gains[layer, 0],
            partial(
                split_attend,
                w_attend=frozen_attend[layer],
                w_output=frozen_output[layer],
                same_seg=same_all,
            ),
        )
        hidden = split_sublayer(
            hidden,
            frozen_gains[layer, 1],
            partial(split_feed, w_expand=frozen_expand[layer], w_reduce=frozen_reduce[layer]),
        )
        tapped = lax.all_to_all(hidden, "head", split_axis=0, concat_axis=2, tiled=True)
        taps.append(tapped.reshape(-1, D))
    return taps


def shards(
    frozen_input,
    frozen_attend,
    frozen_output,
    frozen_expand,
    frozen_reduce,
    frozen_gains,
    lengths,
    side_input,
    cotangent,
    attend_master,
    attend_moment,
    attend_square,
    feed_master,
    feed_moment,
    feed_square,
    down_master,
    down_moment,
    down_square,
    gains_master,
    gains_moment,
    gains_square,
):
    head_count, batch_count = lax.axis_size("head"), lax.axis_size("batch")
    tuned = head_count == 4 and batch_count == 8
    head_at, batch_at = lax.axis_index("head"), lax.axis_index("batch")
    own_rows = lengths.shape[0] // head_count
    place = jnp.stack(
        [
            head_at,
            batch_at % 4,
            head_at % 2,
            head_at // 2 % 2,
            batch_at % 2,
            batch_at // 2 % 2,
            batch_at // 4 % 2,
            batch_at * head_count + head_at,
            jnp.zeros_like(head_at),
            gathered_at(batch_at * head_count + head_at) if tuned else jnp.zeros_like(head_at),
        ]
    ).astype(jnp.int32)
    tokens = own_rows * ROW
    state_in = side_input.reshape(tokens, S)
    frozen = (frozen_attend, frozen_output, frozen_expand, frozen_reduce, frozen_gains)
    masters = (attend_master, feed_master, down_master)
    bias, other_bias, grad_seed, *side_own = prepare(
        lengths, place, cotangent.reshape(tokens, S), masters, tuned
    )
    if tuned:
        taps, whole, (*saved, state) = backbone_rows(
            place,
            frozen_input,
            *frozen,
            (bias, other_bias),
            *side_own,
            lambda tap, whole: side_first(place, tap, whole, state_in, gains_master, bias),
        )
    else:
        mats, feeds, downs = (
            lax.all_gather(array.astype(BF), ("batch", "head"), axis=0, tiled=True)
            for array in masters
        )
        feeds = feeds.reshape(PLACES, -1, SF // S, S).transpose(0, 2, 1, 3)
        whole = jnp.concatenate(
            [array.reshape(PLACES, -1, S) for array in (mats, feeds, downs)], axis=1
        )
        whole = whole.reshape((2,) * 5 + whole.shape[1:]).transpose(4, 0, 1, 2, 3, 5, 6)
        whole = whole.reshape(PLACES, -1, S)
        taps = backbone_split(frozen_input, *frozen, lengths)
        *saved, state = side_first(place, taps[0], whole, state_in, gains_master, bias)
    result, input_grad, *sums = side_last(
        PLACES if tuned else 0,
        place,
        *taps,
        whole,
        state_in,
        state,
        grad_seed,
        gains_master,
        bias,
        saved,
    )
    result = result.reshape(cotangent.shape)
    input_grad = input_grad.reshape(cotangent.shape)
    states = (
        attend_master,
        attend_moment,
        attend_square,
        feed_master,
        feed_moment,
        feed_square,
        down_master,
        down_moment,
        down_square,
        gains_master,
        gains_moment,
        gains_square,
    )
    if tuned:
        kept, sent = sums
        came = swap(sent, "head", 1)
        kept, sent = halve(1, place, kept, came)
        came = swap(sent, "head", 2)
        kept, sent = halve(2, place, kept, came)
        came = swap(sent, "batch", 1)
        kept, sent = halve(3, place, kept, came)
        came = swap(sent, "batch", 2)
        kept, sent = halve(4, place, kept, came)
        came = swap(sent, "batch", 4)
        total, squares = tally(place, kept, came)
        for axis, bit in (("head", 1), ("head", 2), ("batch", 1), ("batch", 2), ("batch", 4)):
            squares = squares + swap(squares, axis, bit)
        grad_norm, *rest = update(total, squares, states)
        return (result, input_grad, grad_norm.reshape(()), *rest)
    grads = lax.psum(tuple(sums), ("batch", "head"))
    grad_norm = jnp.sqrt(sum(jnp.sum(grad * grad) for grad in grads))
    clip = jnp.minimum(1.0, THRESHOLD / grad_norm)
    member = lax.axis_index(("batch", "head"))
    outs = []
    for at, grad in enumerate(grads):
        owned = states[3 * at : 3 * at + 3]
        if at < 3:
            height = owned[0].shape[0]
            grad = lax.dynamic_slice_in_dim(grad, member * height, height, 0)
        rate, decay = (RATE_MATRIX, WEIGHT_DECAY) if at < 3 else (RATE_SMALL, 0.0)
        new = adamw(*owned, grad, clip, rate, decay)
        outs.extend(new)
        if at < 3:
            outs.append(new[0].astype(BF))
    return (result, input_grad, grad_norm, *outs)


def solution(mesh):
    row_split = P(("batch", "head"), None)
    cube_split = P(("batch", "head"), None, None)
    return jax.shard_map(
        shards,
        mesh=mesh,
        in_specs=(
            P("batch", None, "head"),
            P(None, None, None, "head"),
            P(None, "head", None),
            P(None, None, "head"),
            P(None, "head", None),
            P(),
            P("batch", None),
            cube_split,
            cube_split,
        )
        + (row_split,) * 9
        + (P(),) * 3,
        out_specs=(cube_split, cube_split, P()) + (row_split,) * 12 + (P(),) * 3,
        check_vma=False,
    )
```

time: 759 us -> 269 us (0.35)
  waiting for transfers between devices: 377 us -> 110 us
  blocking collectives: 166 us -> 0 us
  Pallas kernels: 0 us -> 113 us
  matrix products: 108 us -> 0 us
  other arithmetic: 52.6 us -> 0.25 us
  starting transfers between devices: 8.47 us -> 37.1 us
  local copies, waits for them, and re-layouts: 21.5 us -> 4.15 us
  between operations: 18.9 us -> 1.58 us
    all_gather x4 -> x0, waiting for transfers between devices: 142 us -> none  [head_sublayer(): whole = lax.all_gather(hidden, 'head', axis=2, tiled=True)]
    reduce_scatter x4 -> x0, waiting for transfers between devices: 134 us -> none  [head_sublayer(): lax.psum_scatter(work(normed).astype(jnp.bfloat16), 'head', scatter_dimen...]
    all_gather x3 -> x0, blocking collectives: 128 us -> none  [the longest x1 48.3 us: shards(): lax.all_gather(attend_master.astype(jnp.bfloat16), ('batch', 'head'), axi...]
    pallas_call x0 -> x34, Pallas kernels: none -> 113 us  [the longest x1 29.6 us: side_last(): pl.pallas_call(partial(side_last_kernel, packed), out_shape=shapes, in_sp...]
    ppermute x0 -> x41, waiting for transfers between devices: none -> 110 us  [swap(): return lax.ppermute(value, axis, [(at, at ^ bit) for at in range(size)])]
    dot_general x48 -> x0, matrix products: 98 us -> none  [the longest x2 26.9 us: feed_part(): jnp.einsum('rtf,fd->rtd', inner, w_reduce, preferred_element_type=jnp.flo...]
    psum x1 -> x0, waiting for transfers between devices: 92.7 us -> none  [shards(): lax.psum((grad_attend, grad_feed, grad_down, grad_gains), ('batch', 'head'))]
    psum x1 -> x0, blocking collectives: 37.2 us -> none  [shards(): lax.psum((grad_attend, grad_feed, grad_down, grad_gains), ('batch', 'head'))]
  transfers between devices with their start and end apart: 11 -> 41, of which waited for: 9 -> 26; matrix products, arithmetic and copies ran while one was open for 3% -> 0% of each run, Pallas kernels for 0% -> 28%
where the time goes in v1:
time: 269 us; the launch traced here: 266 us
  Pallas kernels  113 us (42%)
  waiting for transfers between devices  110 us (41%)
  starting transfers between devices  37.1 us (14%)
  local copies, waits for them, and re-layouts  4.15 us (2%)
    ppermute x41, waiting for transfers between devices, swap(): return lax.ppermute(value, axis, [(at, at ^ bit) for at in range(size)])  110 us
    ppermute x41, starting transfers between devices, swap(): return lax.ppermute(value, axis, [(at, at ^ bit) for at in range(size)])  37.1 us
    pallas_call x1, Pallas kernels, side_last(): pl.pallas_call(partial(side_last_kernel, packed), out_shape=shapes, in_sp...  29.6 us
    pallas_call x4, Pallas kernels, attend_far(): pl.pallas_call(partial(attend_far_kernel, layer), out_shape=shape_of((tok...  16 us
    pallas_call x4, Pallas kernels, feed_own(): pl.pallas_call(partial(feed_kernel, layer), out_shape=sums, in_specs=[VM]...  15.1 us
    pallas_call x4, Pallas kernels, attend_own(): pl.pallas_call(partial(attend_kernel, layer), out_shape=shape_of((tokens,...  14.8 us
    pallas_call x6, Pallas kernels, feed_far_units(): pl.pallas_call(partial(feed_far_kernel, len(parts), sets), out_shape=[sha...  11.4 us
    pallas_call x1, Pallas kernels, side_first(): pl.pallas_call(side_first_kernel, out_shape=[shape_of((tokens, S), kind)...  8.93 us
  transfers between devices with their start and end apart: 41, of which 26 were waited for; matrix products, arithmetic and copies ran while one was open for 0% of the time, Pallas kernels for 28%

profile of v1, /device:TPU:0, one launch (start us, length us, event | category | flops | bytes accessed | tf_op | source)
XLA Modules:
  0.0 265.8 jit_solution(14806293357190890783)
XLA Ops:
  5.9 3.0 %collective-permute-start.2 = (bf16[1,160,128]{2,1,0:T(8,128)(2,1)S(1)}, bf16[1,160,128]{2,1,0:T(8,128)(2,1)S(1)}, u32[]{:S(2)}, u32[]{:S(2)}) collective-permute-start(bf16[1,160,128]{2,1,0:T(8,128)(2,1)S(1)} %get-tuple-element.134), channel_id=1, source_target_pairs={{0,2},{1,3},{2,0},{3,1},{4,6},{5,7},{6,4},{7,5},{8,10},{9,11},{10,... | collective-permute-start | bytes 122888 | tf_op jit(solution)/shard_map/ppermute | solution.py:836
  8.9 3.4 %shard_map.340 = (bf16[8,128,256]{2,1,0:T(8,128)(2,1)}, bf16[8,128,256]{2,1,0:T(8,128)(2,1)}, bf16[4,256,256]{2,1,0:T(8,128)(2,1)}) custom-call(s32[10]{0:T(128)} %copy-done.8, bf16[16,128,256]{2,1,0:T(8,128)(2,1)} %hidden.1, bf16[2,3,1024,256]{3,2,1,0:T(8,128)(2,1)} %weights.7, bf16[2,256,1024]{2,1,0:T(8,128)(2,1)} %out.7), custom_call_target="tpu_custom_call" | custom-call | flops 4000000000 | tf_op jit(solution)/shard_map/pallas_call | solution.py:274
  12.5 2.0 collective-permute-start.3
  14.5 3.1 %collective-permute-done.3 = bf16[2,160,128]{2,1,0:T(8,128)(2,1)S(1)} collective-permute-done((bf16[2,160,128]{2,1,0:T(8,128)(2,1)S(1)}, bf16[2,160,128]{2,1,0:T(8,128)(2,1)S(1)}, u32[]{:S(2)}, u32[]{:S(2)}) %collective-permute-start.3) | collective-permute-done | bytes 81952 | tf_op jit(solution)/shard_map/ppermute | solution.py:836
  17.6 1.9 collective-permute-start.4
  19.5 4.2 %collective-permute-done.4 = bf16[4,160,128]{2,1,0:T(8,128)(2,1)S(1)} collective-permute-done((bf16[4,160,128]{2,1,0:T(8,128)(2,1)S(1)}, bf16[4,160,128]{2,1,0:T(8,128)(2,1)S(1)}, u32[]{:S(2)}, u32[]{:S(2)}) %collective-permute-start.4) | collective-permute-done | bytes 163872 | tf_op jit(solution)/shard_map/ppermute | solution.py:836
  23.7 2.2 collective-permute-done.rest_0_
  26.0 1.6 collective-permute-start.6
  27.6 1.6 collective-permute-start.7
  29.7 2.6 collective-permute-start.8
  32.3 4.8 %shard_map.342 = (bf16[4,256,256]{2,1,0:T(8,128)(2,1)}, bf16[8,256,256]{2,1,0:T(8,128)(2,1)}, bf16[8,256,256]{2,1,0:T(8,128)(2,1)}, bf16[8,256,256]{2,1,0:T(8,128)(2,1)}) custom-call(s32[10]{0:T(128)} %copy-done.8, bf16[2,3,1024,256]{3,2,1,0:T(8,128)(2,1)} %weights.7, bf16[2,256,1024]{2,1,0:T(8,128)(2,1)} %out.7, bf16[2,1024,1024]{2,1,0:T(8,128)(2,1)} %expand.9, ...), custom_call_target="tpu_custom_call" | custom-call | flops 8000000000 | tf_op jit(solution)/shard_map/pallas_call | solution.py:303
  37.1 8.8 %collective-permute-done.8 = bf16[8,160,128]{2,1,0:T(8,128)(2,1)S(1)} collective-permute-done((bf16[8,160,128]{2,1,0:T(8,128)(2,1)S(1)}, bf16[8,160,128]{2,1,0:T(8,128)(2,1)S(1)}, u32[]{:S(2)}, u32[]{:S(2)}) %collective-permute-start.8) | collective-permute-done | bytes 327712 | tf_op jit(solution)/shard_map/ppermute | solution.py:836
  48.7 1.6 shard_map.343
  50.3 4.0 %shard_map.345.context_own = bf16[512,256]{1,0:T(8,128)(2,1)S(1)} custom-call(bf16[512,1024]{1,0:T(8,128)(2,1)S(1)} %get-tuple-element.144.normed, bf16[2,3,1024,256]{3,2,1,0:T(8,128)(2,1)S(1)} %copy-done.19, f32[2,128,256]{2,1,0:T(8,128)S(1)} %get-tuple-element.145.bias), custom_call_target="tpu_custom_call" | custom-call | flops 12000000000 | tf_op jit(solution)/shard_map/pallas_call | solution.py:880
  54.4 3.5 %shard_map.344.context_own = bf16[512,256]{1,0:T(8,128)(2,1)S(1)} custom-call(bf16[512,1024]{1,0:T(8,128)(2,1)S(1)} %get-tuple-element.142.normed, bf16[2,3,1024,256]{3,2,1,0:T(8,128)(2,1)S(1)} %copy-done.19, f32[2,128,256]{2,1,0:T(8,128)S(1)} %get-tuple-element.143.bias), custom_call_target="tpu_custom_call" | custom-call | flops 12000000000 | tf_op jit(solution)/shard_map/pallas_call | solution.py:880
  57.9 3.2 %collective-permute-done.10.rest_3_ = bf16[4,256,256]{2,1,0:T(8,128)(2,1)S(1)} collective-permute-done((bf16[4,256,256]{2,1,0:T(8,128)(2,1)S(1)}, bf16[4,256,256]{2,1,0:T(8,128)(2,1)S(1)}, u32[]{:S(2)}, u32[]{:S(2)}) %collective-permute-start.10) | collective-permute-done | bytes 524320 | tf_op jit(solution)/shard_map/ppermute | solution.py:836
  61.1 4.0 %shard_map.347 = bf16[512,1024]{1,0:T(8,128)(2,1)S(1)} custom-call(s32[10]{0:T(128)S(1)} %copy-done.9, bf16[512,1024]{1,0:T(8,128)(2,1)S(1)} %get-tuple-element.144.normed, f32[2,128,256]{2,1,0:T(8,128)S(1)} %get-tuple-element.145.bias, bf16[512,256]{1,0:T(8,128)(2,1)S(1)} %shard_map.345.context_own, bf16[2,256,1024]{2,1,0:T(8,128)(2,1)S(1)} %copy-done.20, ...), custom_call_target="tpu_custom_call" | custom-call | flops 16000000000 | tf_op jit(solution)/shard_map/pallas_call | solution.py:895
  65.7 4.0 %shard_map.346.total = f32[512,1024]{1,0:T(8,128)S(1)} custom-call(s32[10]{0:T(128)S(1)} %copy-done.9, bf16[512,1024]{1,0:T(8,128)(2,1)S(1)} %get-tuple-element.142.normed, f32[2,128,256]{2,1,0:T(8,128)S(1)} %get-tuple-element.143.bias, bf16[512,256]{1,0:T(8,128)(2,1)S(1)} %shard_map.344.context_own, bf16[2,256,1024]{2,1,0:T(8,128)(2,1)S(1)} %copy-done.20, ...), custom_call_target="tpu_custom_call" | custom-call | flops 16000000000 | tf_op jit(solution)/shard_map/pallas_call | solution.py:895
  70.6 2.2 collective-permute-done.12.refs_4_
  74.3 2.7 %collective-permute-start.17 = (bf16[8,256,256]{2,1,0:T(8,128)(2,1)S(1)}, bf16[8,256,256]{2,1,0:T(8,128)(2,1)S(1)}, u32[]{:S(2)}, u32[]{:S(2)}) collective-permute-start(bf16[8,256,256]{2,1,0:T(8,128)(2,1)S(1)} %collective-permute-done.12.refs_4_), channel_id=1, source_target_pairs={{0,8},{4,12},{8,0},{12,4},{16,24},{20,28},{24,16},{28,20},{1,9},{5... | collective-permute-start | bytes 3145736 | tf_op jit(solution)/shard_map/ppermute | solution.py:836
  77.5 3.8 %shard_map.349.refs_2_ = f32[512,1024]{1,0:T(8,128)S(1)} custom-call(bf16[512,1024]{1,0:T(8,128)(2,1)S(1)} %get-tuple-element.159.normed.refs_0_, bf16[2,1024,1024]{2,1,0:T(8,128)(2,1)S(1)} %copy-done.17, bf16[2,1024,1024]{2,1,0:T(8,128)(2,1)S(1)} %copy-done.18), custom_call_target="tpu_custom_call" | custom-call | flops 12000000000 | tf_op jit(solution)/shard_map/pallas_call | solution.py:923
  81.4 3.6 %shard_map.350.refs_3_ = f32[512,1024]{1,0:T(8,128)S(1)} custom-call(bf16[512,1024]{1,0:T(8,128)(2,1)S(1)} %collective-permute-done.14.normed.refs_1_.refs_0_, bf16[2,1024,1024]{2,1,0:T(8,128)(2,1)S(1)} %copy-done.17, bf16[2,1024,1024]{2,1,0:T(8,128)(2,1)S(1)} %copy-done.18), custom_call_target="tpu_custom_call" | custom-call | flops 12000000000 | tf_op jit(solution)/shard_map/pallas_call | solution.py:923
  85.0 6.3 %collective-permute-done.15.rest_0_ = bf16[4,256,256]{2,1,0:T(8,128)(2,1)S(1)} collective-permute-done((bf16[4,256,256]{2,1,0:T(8,128)(2,1)S(1)}, bf16[4,256,256]{2,1,0:T(8,128)(2,1)S(1)}, u32[]{:S(2)}, u32[]{:S(2)}) %collective-permute-start.15) | collective-permute-done | bytes 524320 | tf_op jit(solution)/shard_map/ppermute | solution.py:836
  91.3 5.9 %collective-permute-done.16.refs_5_ = bf16[8,256,256]{2,1,0:T(8,128)(2,1)S(1)} collective-permute-done((bf16[8,256,256]{2,1,0:T(8,128)(2,1)S(1)}, bf16[8,256,256]{2,1,0:T(8,128)(2,1)S(1)}, u32[]{:S(2)}, u32[]{:S(2)}) %collective-permute-start.16) | collective-permute-done | bytes 1048608 | tf_op jit(solution)/shard_map/ppermute | solution.py:836
  97.3 2.1 collective-permute-done.17.refs_6_
  99.9 1.7 collective-permute-start.19
  102.2 3.6 %shard_map.351 = (f32[512,1024]{1,0:T(8,128)S(1)}, f32[512,1024]{1,0:T(8,128)S(1)}) custom-call(bf16[512,1024]{1,0:T(8,128)(2,1)S(1)} %get-tuple-element.159.normed.refs_0_, bf16[512,1024]{1,0:T(8,128)(2,1)S(1)} %collective-permute-done.14.normed.refs_1_.refs_0_, f32[512,1024]{1,0:T(8,128)S(1)} %shard_map.349.refs_2_, f32[512,1024]{1,0:T(8,128)S(1)} %shard_map.350.refs_3_, ...), custom_call_target="tpu_custom_call" | custom-call | flops 24000000000 | tf_op jit(solution)/shard_map/pallas_call | solution.py:939
  105.7 17.1 %collective-permute-done.18.refs_4_ = bf16[8,256,256]{2,1,0:T(8,128)(2,1)S(1)} collective-permute-done((bf16[8,256,256]{2,1,0:T(8,128)(2,1)S(1)}, bf16[8,256,256]{2,1,0:T(8,128)(2,1)S(1)}, u32[]{:S(2)}, u32[]{:S(2)}) %collective-permute-start.18) | collective-permute-done | bytes 1048608 | tf_op jit(solution)/shard_map/ppermute | solution.py:836
  130.1 3.7 %shard_map.355.context_own = bf16[512,256]{1,0:T(8,128)(2,1)S(1)} custom-call(bf16[512,1024]{1,0:T(8,128)(2,1)S(1)} %get-tuple-element.178.normed, bf16[2,3,1024,256]{3,2,1,0:T(8,128)(2,1)S(1)} %copy-done.19, f32[2,128,256]{2,1,0:T(8,128)S(1)} %get-tuple-element.143.bias), custom_call_target="tpu_custom_call" | custom-call | flops 12000000000 | tf_op jit(solution)/shard_map/pallas_call | solution.py:880
  133.8 3.5 %shard_map.356.context_own = bf16[512,256]{1,0:T(8,128)(2,1)S(1)} custom-call(bf16[512,1024]{1,0:T(8,128)(2,1)S(1)} %collective-permute-done.22.normed, bf16[2,3,1024,256]{3,2,1,0:T(8,128)(2,1)S(1)} %copy-done.19, f32[2,128,256]{2,1,0:T(8,128)S(1)} %get-tuple-element.145.bias), custom_call_target="tpu_custom_call" | custom-call | flops 12000000000 | tf_op jit(solution)/shard_map/pallas_call | solution.py:880
  139.3 8.9 %shard_map.357 = (f32[512,128]{1,0:T(8,128)S(1)}, f32[512,128]{1,0:T(8,128)S(1)}, f32[512,128]{1,0:T(8,128)S(1)}, bf16[512,128]{1,0:T(8,128)(2,1)S(1)}, bf16[512...) custom-call(s32[10]{0:T(128)S(1)} %copy-done.9, ...), custom_call_target="tpu_custom_call" | custom-call | flops 32000000000 | tf_op jit(solution)/shard_map/pallas_call | solution.py:586
  149.8 12.6 %collective-permute-done.24.rest_3_ = bf16[4,256,256]{2,1,0:T(8,128)(2,1)S(1)} collective-permute-done((bf16[4,256,256]{2,1,0:T(8,128)(2,1)S(1)}, bf16[4,256,256]{2,1,0:T(8,128)(2,1)S(1)}, u32[]{:S(2)}, u32[]{:S(2)}) %collective-permute-start.24) | collective-permute-done | bytes 524320 | tf_op jit(solution)/shard_map/ppermute | solution.py:836
  162.4 4.0 %shard_map.359 = bf16[512,1024]{1,0:T(8,128)(2,1)S(1)} custom-call(s32[10]{0:T(128)S(1)} %copy-done.9, bf16[512,1024]{1,0:T(8,128)(2,1)S(1)} %collective-permute-done.22.normed, f32[2,128,256]{2,1,0:T(8,128)S(1)} %get-tuple-element.145.bias, bf16[512,256]{1,0:T(8,128)(2,1)S(1)} %shard_map.356.context_own, bf16[2,256,1024]{2,1,0:T(8,128)(2,1)S(1)} %copy-done.20, ...), custom_call_target="tpu_custom_call" | custom-call | flops 16000000000 | tf_op jit(solution)/shard_map/pallas_call | solution.py:895
  166.5 4.0 %shard_map.358.total = f32[512,1024]{1,0:T(8,128)S(1)} custom-call(s32[10]{0:T(128)S(1)} %copy-done.9, bf16[512,1024]{1,0:T(8,128)(2,1)S(1)} %get-tuple-element.178.normed, f32[2,128,256]{2,1,0:T(8,128)S(1)} %get-tuple-element.143.bias, bf16[512,256]{1,0:T(8,128)(2,1)S(1)} %shard_map.355.context_own, bf16[2,256,1024]{2,1,0:T(8,128)(2,1)S(1)} %copy-done.20, ...), custom_call_target="tpu_custom_call" | custom-call | flops 16000000000 | tf_op jit(solution)/shard_map/pallas_call | solution.py:895
  171.8 4.1 %shard_map.361.refs_2_ = f32[512,1024]{1,0:T(8,128)S(1)} custom-call(bf16[512,1024]{1,0:T(8,128)(2,1)S(1)} %get-tuple-element.196.normed.refs_0_, bf16[2,1024,1024]{2,1,0:T(8,128)(2,1)S(1)} %copy-done.17, bf16[2,1024,1024]{2,1,0:T(8,128)(2,1)S(1)} %copy-done.18), custom_call_target="tpu_custom_call" | custom-call | flops 12000000000 | tf_op jit(solution)/shard_map/pallas_call | solution.py:923
  175.9 3.6 %shard_map.362.refs_3_ = f32[512,1024]{1,0:T(8,128)S(1)} custom-call(bf16[512,1024]{1,0:T(8,128)(2,1)S(1)} %collective-permute-done.26.normed.refs_1_.refs_0_, bf16[2,1024,1024]{2,1,0:T(8,128)(2,1)S(1)} %copy-done.17, bf16[2,1024,1024]{2,1,0:T(8,128)(2,1)S(1)} %copy-done.18), custom_call_target="tpu_custom_call" | custom-call | flops 12000000000 | tf_op jit(solution)/shard_map/pallas_call | solution.py:923
  179.6 2.6 shard_map.363
  186.7 29.6 %shard_map.367 = (f32[512,128]{1,0:T(8,128)}, f32[512,128]{1,0:T(8,128)}, f32[16,176,128]{2,1,0:T(8,128)S(1)}, bf16[16,176,128]{2,1,0:T(8,128)(2,1)S(1)}) custom-call(s32[10]{0:T(128)S(1)} %copy-done.9, bf16[512,1024]{1,0:T(8,128)(2,1)S(1)} %get-tuple-element.177.tap_source.hidden.tap_one, bf16[512,1024]{1,0:T(8,128)(2,1)S(1)} %shard_map.366.tap_two, ...), custom_call_target="tpu_custom_call" | custom-call | flops 120000004096 | tf_op jit(solution)/shard_map/pallas_call | solution.py:732
  216.4 2.1 collective-permute-done.31.came
  220.8 9.0 %collective-permute-done.32.came = bf16[8,176,128]{2,1,0:T(8,128)(2,1)S(1)} collective-permute-done((bf16[8,176,128]{2,1,0:T(8,128)(2,1)S(1)}, bf16[8,176,128]{2,1,0:T(8,128)(2,1)S(1)}, u32[]{:S(2)}, u32[]{:S(2)}) %collective-permute-start.32) | collective-permute-done | bytes 360480 | tf_op jit(solution)/shard_map/ppermute | solution.py:836
  231.0 5.2 %collective-permute-done.33.came = bf16[4,176,128]{2,1,0:T(8,128)(2,1)S(1)} collective-permute-done((bf16[4,176,128]{2,1,0:T(8,128)(2,1)S(1)}, bf16[4,176,128]{2,1,0:T(8,128)(2,1)S(1)}, u32[]{:S(2)}, u32[]{:S(2)}) %collective-permute-start.33) | collective-permute-done | bytes 180256 | tf_op jit(solution)/shard_map/ppermute | solution.py:836
  237.4 4.0 %collective-permute-done.34.came = bf16[2,176,128]{2,1,0:T(8,128)(2,1)S(1)} collective-permute-done((bf16[2,176,128]{2,1,0:T(8,128)(2,1)S(1)}, bf16[2,176,128]{2,1,0:T(8,128)(2,1)S(1)}, u32[]{:S(2)}, u32[]{:S(2)}) %collective-permute-start.34) | collective-permute-done | bytes 90144 | tf_op jit(solution)/shard_map/ppermute | solution.py:836
  242.0 1.7 collective-permute-start.35
  243.7 3.7 %collective-permute-done.35.came = bf16[1,176,128]{2,1,0:T(8,128)(2,1)S(1)} collective-permute-done((bf16[1,176,128]{2,1,0:T(8,128)(2,1)S(1)}, bf16[1,176,128]{2,1,0:T(8,128)(2,1)S(1)}, u32[]{:S(2)}, u32[]{:S(2)}) %collective-permute-start.35) | collective-permute-done | bytes 45088 | tf_op jit(solution)/shard_map/ppermute | solution.py:836
  250.8 2.1 collective-permute-done.37
  253.4 3.1 %collective-permute-done.38 = f32[8,128]{1,0:T(8,128)S(1)} collective-permute-done((f32[8,128]{1,0:T(8,128)S(1)}, f32[8,128]{1,0:T(8,128)S(1)}, u32[]{:S(2)}, u32[]{:S(2)}) %collective-permute-start.38) | collective-permute-done | bytes 4128 | tf_op jit(solution)/shard_map/ppermute | solution.py:836
  256.6 3.5 %collective-permute-done.39 = f32[8,128]{1,0:T(8,128)S(1)} collective-permute-done((f32[8,128]{1,0:T(8,128)S(1)}, f32[8,128]{1,0:T(8,128)S(1)}, u32[]{:S(2)}, u32[]{:S(2)}) %collective-permute-start.39) | collective-permute-done | bytes 4128 | tf_op jit(solution)/shard_map/ppermute | solution.py:836
  261.3 3.3 %collective-permute-done.40 = f32[8,128]{1,0:T(8,128)S(1)} collective-permute-done((f32[8,128]{1,0:T(8,128)S(1)}, f32[8,128]{1,0:T(8,128)S(1)}, u32[]{:S(2)}, u32[]{:S(2)}) %collective-permute-start.40) | collective-permute-done | bytes 4128 | tf_op jit(solution)/shard_map/ppermute | solution.py:836
  (136 shorter events, 41.2 us)
Async XLA Ops:
  5.9 6.5 %collective-permute-start.2 = (bf16[1,160,128]{2,1,0:T(8,128)(2,1)S(1)}, bf16[1,160,128]{2,1,0:T(8,128)(2,1)S(1)}, u32[]{:S(2)}, u32[]{:S(2)}) collective-permute-start(bf16[1,160,128]{2,1,0:T(8,128)(2,1)S(1)} %get-tuple-element.134), channel_id=1, source_target_pairs={{0,2},{1,3},{2,0},{3,1},{4,6},{5,7},{6,4},{7,5},{8,10},{9,11},{10,... | collective-permute-start | bytes 122888 | tf_op jit(solution)/shard_map/ppermute | solution.py:836
  12.3 13.7 %collective-permute-start = (bf16[4,256,256]{2,1,0:T(8,128)(2,1)}, bf16[4,256,256]{2,1,0:T(8,128)(2,1)S(1)}, u32[]{:S(2)}, u32[]{:S(2)}) collective-permute-start(bf16[4,256,256]{2,1,0:T(8,128)(2,1)} %get-tuple-element.132), channel_id=1, source_target_pairs={{0,2},{1,3},{2,0},{3,1},{4,6},{5,7},{6,4},{7,5},{8,10},{9,11},{10,... | collective-permute-start | bytes 1572872 | tf_op jit(solution)/shard_map/ppermute | solution.py:836
  12.4 13.6 %collective-permute-start.1 = (bf16[8,128,256]{2,1,0:T(8,128)(2,1)}, bf16[8,128,256]{2,1,0:T(8,128)(2,1)S(1)}, u32[]{:S(2)}, u32[]{:S(2)}) collective-permute-start(bf16[8,128,256]{2,1,0:T(8,128)(2,1)} %get-tuple-element.131.own), channel_id=1, source_target_pairs={{0,1},{1,0},{2,3},{3,2},{4,5},{5,4},{6,7},{7,6},{8,9},{9,8},{10,11... | collective-permute-start | bytes 1572872 | tf_op jit(solution)/shard_map/ppermute | solution.py:836
  12.5 5.1 %collective-permute-start.3 = (bf16[2,160,128]{2,1,0:T(8,128)(2,1)S(1)}, bf16[2,160,128]{2,1,0:T(8,128)(2,1)S(1)}, u32[]{:S(2)}, u32[]{:S(2)}) collective-permute-start(bf16[2,160,128]{2,1,0:T(8,128)(2,1)S(1)} %pad_maximum_fusion.4), channel_id=1, source_target_pairs={{0,4},{4,0},{8,12},{12,8},{16,20},{20,16},{24,28},{28,24},{1,5},{5... | collective-permute-start | bytes 245768 | tf_op jit(solution)/shard_map/ppermute | solution.py:836
  17.6 6.0 %collective-permute-start.4 = (bf16[4,160,128]{2,1,0:T(8,128)(2,1)S(1)}, bf16[4,160,128]{2,1,0:T(8,128)(2,1)S(1)}, u32[]{:S(2)}, u32[]{:S(2)}) collective-permute-start(bf16[4,160,128]{2,1,0:T(8,128)(2,1)S(1)} %pad_maximum_fusion.3), channel_id=1, source_target_pairs={{0,8},{4,12},{8,0},{12,4},{16,24},{20,28},{24,16},{28,20},{1,9},{5... | collective-permute-start | bytes 491528 | tf_op jit(solution)/shard_map/ppermute | solution.py:836
  26.0 19.9 %collective-permute-start.6 = (bf16[4,256,256]{2,1,0:T(8,128)(2,1)S(1)}, bf16[4,256,256]{2,1,0:T(8,128)(2,1)S(1)}, u32[]{:S(2)}, u32[]{:S(2)}) collective-permute-start(bf16[4,256,256]{2,1,0:T(8,128)(2,1)S(1)} %collective-permute-done.rest_0_), channel_id=1, source_target_pairs={{0,4},{4,0},{8,12},{12,8},{16,20},{20,16},{24,28},{28,24},{1,5},{5... | collective-permute-start | bytes 1572872 | tf_op jit(solution)/shard_map/ppermute | solution.py:836
  27.6 19.2 %collective-permute-start.7 = (bf16[4,256,256]{2,1,0:T(8,128)(2,1)S(1)}, bf16[4,256,256]{2,1,0:T(8,128)(2,1)S(1)}, u32[]{:S(2)}, u32[]{:S(2)}) collective-permute-start(bf16[4,256,256]{2,1,0:T(8,128)(2,1)S(1)} %collective-permute-done.rest_0_), channel_id=1, source_target_pairs={{0,8},{4,12},{8,0},{12,4},{16,24},{20,28},{24,16},{28,20},{1,9},{5... | collective-permute-start | bytes 1572872 | tf_op jit(solution)/shard_map/ppermute | solution.py:836
  29.1 16.7 %collective-permute-start.5 = (bf16[8,128,256]{2,1,0:T(8,128)(2,1)}, bf16[8,128,256]{2,1,0:T(8,128)(2,1)S(1)}, u32[]{:S(2)}, u32[]{:S(2)}) collective-permute-start(bf16[8,128,256]{2,1,0:T(8,128)(2,1)} %get-tuple-element.136), channel_id=1, source_target_pairs={{0,2},{1,3},{2,0},{3,1},{4,6},{5,7},{6,4},{7,5},{8,10},{9,11},{10,... | collective-permute-start | bytes 1572872 | tf_op jit(solution)/shard_map/ppermute | solution.py:836
  29.7 16.2 %collective-permute-start.8 = (bf16[8,160,128]{2,1,0:T(8,128)(2,1)S(1)}, bf16[8,160,128]{2,1,0:T(8,128)(2,1)S(1)}, u32[]{:S(2)}, u32[]{:S(2)}) collective-permute-start(bf16[8,160,128]{2,1,0:T(8,128)(2,1)S(1)} %pad_maximum_fusion.2), channel_id=1, source_target_pairs={{0,16},{4,20},{8,24},{12,28},{16,0},{20,4},{24,8},{28,12},{1,17},{... | collective-permute-start | bytes 983048 | tf_op jit(solution)/shard_map/ppermute | solution.py:836
  46.8 1.9 collective-permute-start.9
  46.8 14.3 %collective-permute-start.10 = (bf16[4,256,256]{2,1,0:T(8,128)(2,1)S(1)}, bf16[4,256,256]{2,1,0:T(8,128)(2,1)S(1)}, u32[]{:S(2)}, u32[]{:S(2)}) collective-permute-start(bf16[4,256,256]{2,1,0:T(8,128)(2,1)S(1)} %collective-permute-done.7.rest_2_), channel_id=1, source_target_pairs={{0,4},{4,0},{8,12},{12,8},{16,20},{20,16},{24,28},{28,24},{1,5},{5... | collective-permute-start | bytes 1572872 | tf_op jit(solution)/shard_map/ppermute | solution.py:836
  47.3 25.5 %collective-permute-start.12 = (bf16[8,256,256]{2,1,0:T(8,128)(2,1)}, bf16[8,256,256]{2,1,0:T(8,128)(2,1)S(1)}, u32[]{:S(2)}, u32[]{:S(2)}) collective-permute-start(bf16[8,256,256]{2,1,0:T(8,128)(2,1)} %get-tuple-element.155), channel_id=1, source_target_pairs={{0,2},{1,3},{2,0},{3,1},{4,6},{5,7},{6,4},{7,5},{8,10},{9,11},{10,... | collective-permute-start | bytes 3145736 | tf_op jit(solution)/shard_map/ppermute | solution.py:836
  61.1 8.6 %collective-permute-start.13 = (bf16[16,160,128]{2,1,0:T(8,128)(2,1)S(1)}, bf16[16,160,128]{2,1,0:T(8,128)(2,1)S(1)}, u32[]{:S(2)}, u32[]{:S(2)}) collective-permute-start(bf16[16,160,128]{2,1,0:T(8,128)(2,1)S(1)} %pad_maximum_fusion.1), channel_id=1, source_target_pairs={{0,1},{1,0},{2,3},{3,2},{4,5},{5,4},{6,7},{7,6},{8,9},{9,8},{10,11... | collective-permute-start | bytes 1966088 | tf_op jit(solution)/shard_map/ppermute | solution.py:836
  65.1 4.7 %collective-permute-start.11 = (bf16[512,1024]{1,0:T(8,128)(2,1)S(1)}, bf16[512,1024]{1,0:T(8,128)(2,1)S(1)}, u32[]{:S(2)}, u32[]{:S(2)}) collective-permute-start(bf16[512,1024]{1,0:T(8,128)(2,1)S(1)} %shard_map.347), channel_id=1, source_target_pairs={{0,1},{1,0},{2,3},{3,2},{4,5},{5,4},{6,7},{7,6},{8,9},{9,8},{10,11... | collective-permute-start | bytes 3145736 | tf_op jit(solution)/shard_map/ppermute | solution.py:836
  72.8 24.5 %collective-permute-start.16 = (bf16[8,256,256]{2,1,0:T(8,128)(2,1)S(1)}, bf16[8,256,256]{2,1,0:T(8,128)(2,1)S(1)}, u32[]{:S(2)}, u32[]{:S(2)}) collective-permute-start(bf16[8,256,256]{2,1,0:T(8,128)(2,1)S(1)} %collective-permute-done.12.refs_4_), channel_id=1, source_target_pairs={{0,4},{4,0},{8,12},{12,8},{16,20},{20,16},{24,28},{28,24},{1,5},{5... | collective-permute-start | bytes 3145736 | tf_op jit(solution)/shard_map/ppermute | solution.py:836
  74.3 25.1 %collective-permute-start.17 = (bf16[8,256,256]{2,1,0:T(8,128)(2,1)S(1)}, bf16[8,256,256]{2,1,0:T(8,128)(2,1)S(1)}, u32[]{:S(2)}, u32[]{:S(2)}) collective-permute-start(bf16[8,256,256]{2,1,0:T(8,128)(2,1)S(1)} %collective-permute-done.12.refs_4_), channel_id=1, source_target_pairs={{0,8},{4,12},{8,0},{12,4},{16,24},{20,28},{24,16},{28,20},{1,9},{5... | collective-permute-start | bytes 3145736 | tf_op jit(solution)/shard_map/ppermute | solution.py:836
  77.0 4.4 %collective-permute-start.14 = (bf16[512,1024]{1,0:T(8,128)(2,1)S(1)}, bf16[512,1024]{1,0:T(8,128)(2,1)S(1)}, u32[]{:S(2)}, u32[]{:S(2)}) collective-permute-start(bf16[512,1024]{1,0:T(8,128)(2,1)S(1)} %get-tuple-element.159.normed.refs_0_), channel_id=1, source_target_pairs={{0,1},{1,0},{2,3},{3,2},{4,5},{5,4},{6,7},{7,6},{8,9},{9,8},{10,11... | collective-permute-start | bytes 3145736 | tf_op jit(solution)/shard_map/ppermute | solution.py:836
  77.0 14.3 %collective-permute-start.15 = (bf16[4,256,256]{2,1,0:T(8,128)(2,1)S(1)}, bf16[4,256,256]{2,1,0:T(8,128)(2,1)S(1)}, u32[]{:S(2)}, u32[]{:S(2)}) collective-permute-start(bf16[4,256,256]{2,1,0:T(8,128)(2,1)S(1)} %copy-done.27), channel_id=1, source_target_pairs={{0,2},{1,3},{2,0},{3,1},{4,6},{5,7},{6,4},{7,5},{8,10},{9,11},{10,... | collective-permute-start | bytes 1572872 | tf_op jit(solution)/shard_map/ppermute | solution.py:836
  99.4 23.5 %collective-permute-start.18 = (bf16[8,256,256]{2,1,0:T(8,128)(2,1)S(1)}, bf16[8,256,256]{2,1,0:T(8,128)(2,1)S(1)}, u32[]{:S(2)}, u32[]{:S(2)}) collective-permute-start(bf16[8,256,256]{2,1,0:T(8,128)(2,1)S(1)} %copy-done.26), channel_id=1, source_target_pairs={{0,2},{1,3},{2,0},{3,1},{4,6},{5,7},{6,4},{7,5},{8,10},{9,11},{10,... | collective-permute-start | bytes 3145736 | tf_op jit(solution)/shard_map/ppermute | solution.py:836
  99.9 23.2 %collective-permute-start.19 = (bf16[8,256,256]{2,1,0:T(8,128)(2,1)S(1)}, bf16[8,256,256]{2,1,0:T(8,128)(2,1)S(1)}, u32[]{:S(2)}, u32[]{:S(2)}) collective-permute-start(bf16[8,256,256]{2,1,0:T(8,128)(2,1)S(1)} %collective-permute-done.16.refs_5_), channel_id=1, source_target_pairs={{0,8},{4,12},{8,0},{12,4},{16,24},{20,28},{24,16},{28,20},{1,9},{5... | collective-permute-start | bytes 3145736 | tf_op jit(solution)/shard_map/ppermute | solution.py:836
  101.7 21.2 %collective-permute-start.20 = (bf16[4,256,256]{2,1,0:T(8,128)(2,1)S(1)}, bf16[4,256,256]{2,1,0:T(8,128)(2,1)S(1)}, u32[]{:S(2)}, u32[]{:S(2)}) collective-permute-start(bf16[4,256,256]{2,1,0:T(8,128)(2,1)S(1)} %collective-permute-done.15.rest_0_), channel_id=1, source_target_pairs={{0,4},{4,0},{8,12},{12,8},{16,20},{20,16},{24,28},{28,24},{1,5},{5... | collective-permute-start | bytes 1572872 | tf_op jit(solution)/shard_map/ppermute | solution.py:836
  124.4 4.9 %collective-permute-start.21 = (bf16[512,1024]{1,0:T(8,128)(2,1)S(1)}, bf16[512,1024]{1,0:T(8,128)(2,1)S(1)}, u32[]{:S(2)}, u32[]{:S(2)}) collective-permute-start(bf16[512,1024]{1,0:T(8,128)(2,1)S(1)} %shard_map.353), channel_id=1, source_target_pairs={{0,1},{1,0},{2,3},{3,2},{4,5},{5,4},{6,7},{7,6},{8,9},{9,8},{10,11... | collective-permute-start | bytes 3145736 | tf_op jit(solution)/shard_map/ppermute | solution.py:836
  124.4 14.3 %collective-permute-start.23 = (bf16[4,256,256]{2,1,0:T(8,128)(2,1)S(1)}, bf16[4,256,256]{2,1,0:T(8,128)(2,1)S(1)}, u32[]{:S(2)}, u32[]{:S(2)}) collective-permute-start(bf16[4,256,256]{2,1,0:T(8,128)(2,1)S(1)} %collective-permute-done.15.rest_0_), channel_id=1, source_target_pairs={{0,8},{4,12},{8,0},{12,4},{16,24},{20,28},{24,16},{28,20},{1,9},{5... | collective-permute-start | bytes 1572872 | tf_op jit(solution)/shard_map/ppermute | solution.py:836
  126.0 53.6 %collective-permute-start.27 = (bf16[8,256,256]{2,1,0:T(8,128)(2,1)S(1)}, bf16[8,256,256]{2,1,0:T(8,128)(2,1)S(1)}, u32[]{:S(2)}, u32[]{:S(2)}) collective-permute-start(bf16[8,256,256]{2,1,0:T(8,128)(2,1)S(1)} %collective-permute-done.18.refs_4_), channel_id=1, source_target_pairs={{0,4},{4,0},{8,12},{12,8},{16,20},{20,16},{24,28},{28,24},{1,5},{5... | collective-permute-start | bytes 3145736 | tf_op jit(solution)/shard_map/ppermute | solution.py:836
  126.5 55.7 %collective-permute-start.28 = (bf16[8,256,256]{2,1,0:T(8,128)(2,1)S(1)}, bf16[8,256,256]{2,1,0:T(8,128)(2,1)S(1)}, u32[]{:S(2)}, u32[]{:S(2)}) collective-permute-start(bf16[8,256,256]{2,1,0:T(8,128)(2,1)S(1)} %copy-done.25), channel_id=1, source_target_pairs={{0,2},{1,3},{2,0},{3,1},{4,6},{5,7},{6,4},{7,5},{8,10},{9,11},{10,... | collective-permute-start | bytes 3145736 | tf_op jit(solution)/shard_map/ppermute | solution.py:836
  130.0 3.8 %collective-permute-start.22 = (bf16[512,1024]{1,0:T(8,128)(2,1)S(1)}, bf16[512,1024]{1,0:T(8,128)(2,1)S(1)}, u32[]{:S(2)}, u32[]{:S(2)}) collective-permute-start(bf16[512,1024]{1,0:T(8,128)(2,1)S(1)} %get-tuple-element.178.normed), channel_id=1, source_target_pairs={{0,1},{1,0},{2,3},{3,2},{4,5},{5,4},{6,7},{7,6},{8,9},{9,8},{10,11... | collective-permute-start | bytes 3145736 | tf_op jit(solution)/shard_map/ppermute | solution.py:836
  138.8 23.7 %collective-permute-start.24 = (bf16[4,256,256]{2,1,0:T(8,128)(2,1)S(1)}, bf16[4,256,256]{2,1,0:T(8,128)(2,1)S(1)}, u32[]{:S(2)}, u32[]{:S(2)}) collective-permute-start(bf16[4,256,256]{2,1,0:T(8,128)(2,1)S(1)} %collective-permute-done.23.rest_2_), channel_id=1, source_target_pairs={{0,4},{4,0},{8,12},{12,8},{16,20},{20,16},{24,28},{28,24},{1,5},{5... | collective-permute-start | bytes 1572872 | tf_op jit(solution)/shard_map/ppermute | solution.py:836
  148.2 34.0 %collective-permute-start.29 = (bf16[8,256,256]{2,1,0:T(8,128)(2,1)S(1)}, bf16[8,256,256]{2,1,0:T(8,128)(2,1)S(1)}, u32[]{:S(2)}, u32[]{:S(2)}) collective-permute-start(bf16[8,256,256]{2,1,0:T(8,128)(2,1)S(1)} %collective-permute-done.18.refs_4_), channel_id=1, source_target_pairs={{0,8},{4,12},{8,0},{12,4},{16,24},{20,28},{24,16},{28,20},{1,9},{5... | collective-permute-start | bytes 3145736 | tf_op jit(solution)/shard_map/ppermute | solution.py:836
  166.5 4.1 %collective-permute-start.25 = (bf16[512,1024]{1,0:T(8,128)(2,1)S(1)}, bf16[512,1024]{1,0:T(8,128)(2,1)S(1)}, u32[]{:S(2)}, u32[]{:S(2)}) collective-permute-start(bf16[512,1024]{1,0:T(8,128)(2,1)S(1)} %shard_map.359), channel_id=1, source_target_pairs={{0,1},{1,0},{2,3},{3,2},{4,5},{5,4},{6,7},{7,6},{8,9},{9,8},{10,11... | collective-permute-start | bytes 3145736 | tf_op jit(solution)/shard_map/ppermute | solution.py:836
  171.3 4.6 %collective-permute-start.26 = (bf16[512,1024]{1,0:T(8,128)(2,1)S(1)}, bf16[512,1024]{1,0:T(8,128)(2,1)S(1)}, u32[]{:S(2)}, u32[]{:S(2)}) collective-permute-start(bf16[512,1024]{1,0:T(8,128)(2,1)S(1)} %get-tuple-element.196.normed.refs_0_), channel_id=1, source_target_pairs={{0,1},{1,0},{2,3},{3,2},{4,5},{5,4},{6,7},{7,6},{8,9},{9,8},{10,11... | collective-permute-start | bytes 3145736 | tf_op jit(solution)/shard_map/ppermute | solution.py:836
  183.6 2.7 %collective-permute-start.30 = (bf16[512,1024]{1,0:T(8,128)(2,1)S(1)}, bf16[512,1024]{1,0:T(8,128)(2,1)S(1)}, u32[]{:S(2)}, u32[]{:S(2)}) collective-permute-start(bf16[512,1024]{1,0:T(8,128)(2,1)S(1)} %shard_map.365), channel_id=1, source_target_pairs={{0,1},{1,0},{2,3},{3,2},{4,5},{5,4},{6,7},{7,6},{8,9},{9,8},{10,11... | collective-permute-start | bytes 3145736 | tf_op jit(solution)/shard_map/ppermute | solution.py:836
  216.3 2.2 collective-permute-start.31
  218.5 46.1 %copy-start.5 = (f32[16,512]{1,0:T(8,128)S(1)}, f32[16,512]{1,0:T(8,128)}, u32[]{:S(2)}) copy-start(f32[16,512]{1,0:T(8,128)} %refs_5_.1) | copy-start | bytes 98308
  218.5 46.1 %copy-start.6 = (f32[64,128]{1,0:T(8,128)S(1)}, f32[64,128]{1,0:T(8,128)}, u32[]{:S(2)}) copy-start(f32[64,128]{1,0:T(8,128)} %refs_7_.1) | copy-start | bytes 98308
  218.5 46.1 %copy-start.7 = (f32[64,128]{1,0:T(8,128)S(1)}, f32[64,128]{1,0:T(8,128)}, u32[]{:S(2)}) copy-start(f32[64,128]{1,0:T(8,128)} %refs_8_.1) | copy-start | bytes 98308
  218.5 46.1 %copy-start.11 = (f32[32,128]{1,0:T(8,128)S(1)}, f32[32,128]{1,0:T(8,128)}, u32[]{:S(2)}) copy-start(f32[32,128]{1,0:T(8,128)} %refs_0_.1) | copy-start | bytes 49156
  218.6 46.1 %copy-start.12 = (f32[32,128]{1,0:T(8,128)S(1)}, f32[32,128]{1,0:T(8,128)}, u32[]{:S(2)}) copy-start(f32[32,128]{1,0:T(8,128)} %refs_1_.1) | copy-start | bytes 49156
  218.6 46.1 %copy-start.13 = (f32[32,128]{1,0:T(8,128)S(1)}, f32[32,128]{1,0:T(8,128)}, u32[]{:S(2)}) copy-start(f32[32,128]{1,0:T(8,128)} %refs_2_.1) | copy-start | bytes 49156
  218.6 46.1 %copy-start.15 = (f32[6,128]{1,0:T(8,128)S(1)}, f32[6,128]{1,0:T(8,128)}, u32[]{:S(2)}) copy-start(f32[6,128]{1,0:T(8,128)} %refs_10_.1) | copy-start | bytes 9220
  219.3 10.5 %collective-permute-start.32 = (bf16[8,176,128]{2,1,0:T(8,128)(2,1)S(1)}, bf16[8,176,128]{2,1,0:T(8,128)(2,1)S(1)}, u32[]{:S(2)}, u32[]{:S(2)}) collective-permute-start(bf16[8,176,128]{2,1,0:T(8,128)(2,1)S(1)} %get-tuple-element.219), channel_id=1, source_target_pairs={{0,2},{1,3},{2,0},{3,1},{4,6},{5,7},{6,4},{7,5},{8,10},{9,11},{10,... | collective-permute-start | bytes 1081352 | tf_op jit(solution)/shard_map/ppermute | solution.py:836
  230.4 5.8 %collective-permute-start.33 = (bf16[4,176,128]{2,1,0:T(8,128)(2,1)S(1)}, bf16[4,176,128]{2,1,0:T(8,128)(2,1)S(1)}, u32[]{:S(2)}, u32[]{:S(2)}) collective-permute-start(bf16[4,176,128]{2,1,0:T(8,128)(2,1)S(1)} %get-tuple-element.221), channel_id=1, source_target_pairs={{0,4},{4,0},{8,12},{12,8},{16,20},{20,16},{24,28},{28,24},{1,5},{5... | collective-permute-start | bytes 540680 | tf_op jit(solution)/shard_map/ppermute | solution.py:836
  236.8 4.6 %collective-permute-start.34 = (bf16[2,176,128]{2,1,0:T(8,128)(2,1)S(1)}, bf16[2,176,128]{2,1,0:T(8,128)(2,1)S(1)}, u32[]{:S(2)}, u32[]{:S(2)}) collective-permute-start(bf16[2,176,128]{2,1,0:T(8,128)(2,1)S(1)} %get-tuple-element.223), channel_id=1, source_target_pairs={{0,8},{4,12},{8,0},{12,4},{16,24},{20,28},{24,16},{28,20},{1,9},{5... | collective-permute-start | bytes 270344 | tf_op jit(solution)/shard_map/ppermute | solution.py:836
  242.0 5.5 %collective-permute-start.35 = (bf16[1,176,128]{2,1,0:T(8,128)(2,1)S(1)}, bf16[1,176,128]{2,1,0:T(8,128)(2,1)S(1)}, u32[]{:S(2)}, u32[]{:S(2)}) collective-permute-start(bf16[1,176,128]{2,1,0:T(8,128)(2,1)S(1)} %get-tuple-element.225), channel_id=1, source_target_pairs={{0,16},{4,20},{8,24},{12,28},{16,0},{20,4},{24,8},{28,12},{1,17},{... | collective-permute-start | bytes 135176 | tf_op jit(solution)/shard_map/ppermute | solution.py:836
  248.0 1.2 collective-permute-start.36
  249.2 3.6 %collective-permute-start.37 = (f32[8,128]{1,0:T(8,128)S(1)}, f32[8,128]{1,0:T(8,128)S(1)}, u32[]{:S(2)}, u32[]{:S(2)}) collective-permute-start(f32[8,128]{1,0:T(8,128)S(1)} %add.64), channel_id=1, source_target_pairs={{0,2},{1,3},{2,0},{3,1},{4,6},{5,7},{6,4},{7,5},{8,10},{9,11},{10,... | collective-permute-start | bytes 12296 | tf_op jit(solution)/shard_map/ppermute | solution.py:836
  252.9 3.6 %collective-permute-start.38 = (f32[8,128]{1,0:T(8,128)S(1)}, f32[8,128]{1,0:T(8,128)S(1)}, u32[]{:S(2)}, u32[]{:S(2)}) collective-permute-start(f32[8,128]{1,0:T(8,128)S(1)} %add.65), channel_id=1, source_target_pairs={{0,4},{4,0},{8,12},{12,8},{16,20},{20,16},{24,28},{28,24},{1,5},{5... | collective-permute-start | bytes 12296 | tf_op jit(solution)/shard_map/ppermute | solution.py:836
  256.5 3.6 %collective-permute-start.39 = (f32[8,128]{1,0:T(8,128)S(1)}, f32[8,128]{1,0:T(8,128)S(1)}, u32[]{:S(2)}, u32[]{:S(2)}) collective-permute-start(f32[8,128]{1,0:T(8,128)S(1)} %add.66), channel_id=1, source_target_pairs={{0,8},{4,12},{8,0},{12,4},{16,24},{20,28},{24,16},{28,20},{1,9},{5... | collective-permute-start | bytes 12296 | tf_op jit(solution)/shard_map/ppermute | solution.py:836
  260.1 4.5 %collective-permute-start.40 = (f32[8,128]{1,0:T(8,128)S(1)}, f32[8,128]{1,0:T(8,128)S(1)}, u32[]{:S(2)}, u32[]{:S(2)}) collective-permute-start(f32[8,128]{1,0:T(8,128)S(1)} %add.67), channel_id=1, source_target_pairs={{0,16},{4,20},{8,24},{12,28},{16,0},{20,4},{24,8},{28,12},{1,17},{... | collective-permute-start | bytes 12296 | tf_op jit(solution)/shard_map/ppermute | solution.py:836
  (21 other events, 324.3 us)
